TPU v7x, 512 devices: a whole 4x8x8 slice. The times are simulated.
512 devices in a mesh: inter: 16 (over z_lo, x, core), intra: 32 (over z_hi, y).
Axes of the slice: x: 4, y: 8, z: 8 (z_hi: 4, z_lo: 2; z = z_hi * 2 + z_lo), core: 2. Of those that a mesh axis runs over, the one named last changes fastest.
Arguments:
- hidden: bfloat16 [8192, 14336], P('intra', 'inter'), may hold values from -6 to 6
- cotangent: bfloat16 [8192, 4096], P('intra'), may hold values from -6 to 6
- packed_codes: int32 [3584, 4096], P('inter', 'intra'), may hold values from 0 to 65535
- block_scales: float32 [112, 32], P('inter', 'intra'), may hold values from 0.0006 to 0.006
Outputs:
- output: bfloat16 [8192, 4096], P(('intra', 'inter'))
- grad_hidden: bfloat16 [8192, 14336], P('intra', 'inter')
- grad_weight: float32 [14336, 4096], P('inter', 'intra')
All inputs are finite; a program needn't handle non-finite values.
Results may differ from a plain program's by a relative error of at most 0.022.
Values may be sent and summed in bfloat16 or wider, within the bound.
No kernel may reach another device: no remote copies, remote signals or barrier semaphores. Data moves between devices by JAX's collectives and lax.ppermute only.
A program may use at most 128 MiB of HBM per device.

v0:
```python
import jax
import jax.numpy as jnp
from jax import lax
from jax.sharding import PartitionSpec as P


def unpack_weight(packed_codes, block_scales):
    layers = [
        jnp.bitwise_and(jnp.right_shift(packed_codes, 4 * nibble_slot), 15) - 8
        for nibble_slot in range(4)
    ]
    stacked = jnp.stack(layers, axis=1)
    unpacked = stacked.reshape(-1, packed_codes.shape[1]).astype(jnp.float32)
    row_total, col_total = unpacked.shape
    scale_rows, scale_cols = block_scales.shape
    blocked = unpacked.reshape(
        scale_rows, row_total // scale_rows, scale_cols, col_total // scale_cols
    )
    scaled = blocked * block_scales[:, None, :, None]
    return scaled.reshape(row_total, col_total).astype(jnp.bfloat16)


def per_device(hidden, cotangent, packed_codes, block_scales):
    all_codes = lax.all_gather(packed_codes, "intra", axis=1, tiled=True)
    all_scales = lax.all_gather(block_scales, "intra", axis=1, tiled=True)
    weight = unpack_weight(all_codes, all_scales)
    output = lax.psum_scatter(
        jnp.dot(hidden, weight, preferred_element_type=jnp.float32).astype(jnp.bfloat16),
        "inter",
        scatter_dimension=0,
        tiled=True,
    )
    grad_hidden = lax.dot_general(
        cotangent, weight, (((1,), (1,)), ((), ())), preferred_element_type=jnp.float32
    ).astype(jnp.bfloat16)
    group_count = lax.axis_size("intra")
    grad_term = lax.dot_general(
        hidden, cotangent, (((0,), (0,)), ((), ())), preferred_element_type=jnp.float32
    ).astype(jnp.bfloat16)
    received = lax.all_to_all(grad_term, "intra", split_axis=1, concat_axis=0, tiled=True)
    pieces = received.reshape(group_count, grad_term.shape[0], received.shape[1])
    grad_weight = jnp.sum(pieces.astype(jnp.float32), axis=0)
    return (output, grad_hidden, grad_weight)


def solution(mesh):
    in_specs = (P("intra", "inter"), P("intra", None), P("inter", "intra"), P("inter", "intra"))
    out_specs = (P(("intra", "inter"), None), P("intra", "inter"), P("inter", "intra"))
    return jax.shard_map(
        per_device, mesh=mesh, in_specs=in_specs, out_specs=out_specs, check_vma=False
    )
```

profile of v0, /device:TPU:1, one launch (start us, length us, event | category | flops | bytes accessed | tf_op | source)
XLA Modules:
  0.0 499.2 jit_solution(15108588345618230975)
XLA Ops:
  7.2 0.0 copy-start
  7.2 0.0 all-gather.3.cloned.1.call-start
  7.2 0.7 all-gather.3.cloned.1.call-update
  7.9 0.8 copy-done
  8.8 3.1 convert_bitcast_fusion
  11.9 5.1 %copy.25 = bf16[112,32,8,128]{3,2,0,1:T(8,128)(2,1)} copy(bf16[112,32,8,128]{3,2,1,0:T(8,128)(2,1)S(1)} %convert_bitcast_fusion) | data formatting | bytes 14680064 | tf_op jit(solution)/shard_map/all_to_all | solution.py:40
  16.9 0.0 copy-start.4
  16.9 16.8 %all-to-all-start = ((bf16[896,32,128]{2,0,1:T(8,128)(2,1)}), bf16[896,32,128]{2,0,1:T(8,128)(2,1)}, u32[]{:S(2)}, u32[]{:S(2)}) async-start(bf16[896,32,128]{2,0,1:T(8,128)(2,1)} %bitcast.35), calls=%async_computation | async-start | bytes 14680064 | tf_op jit(solution)/shard_map/all_to_all | solution.py:40
  33.7 0.0 reduce-scatter.4.cloned.1.call-start
  33.8 0.0 copy-done.4
  33.8 297.7 %all-gather = f32[32,1,7]{2,1,0:T(1,128)S(1)} all-gather(f32[1,1,7]{2,1,0:T(1,128)S(1)} %bitcast.37), channel_id=1, replica_groups=mesh['inter'=16,'intra'=32] {'intra'}, dimensions={0}, use_global_device_ids=true | all-gather | bytes 924 | tf_op jit(solution)/shard_map/all_gather | solution.py:25
  331.5 0.1 copy.15
  331.5 0.0 all-gather.3.cloned.1.call-done
  331.5 4.1 add_bitcast_fusion.3
  335.6 1.4 add_convert_fusion
  337.0 16.7 %copy.14 = f32[224,4,4096]{2,1,0:T(4,128)} copy(f32[224,4,4096]{2,0,1:T(8,128)S(1)} %add_convert_fusion) | data formatting | bytes 29360128 | tf_op jit(solution)/shard_map/convert_element_type | solution.py:13
  353.7 17.0 %convert_element_type.31 = f32[896,4096]{1,0:T(8,128)} reshape(f32[224,4,4096]{2,1,0:T(4,128)} %copy.14) | data formatting | bytes 29360128 | tf_op jit(solution)/shard_map/convert_element_type | solution.py:13
  370.7 0.0 copy-start.1
  370.7 9.4 %mul.11 = f32[7,128,32,128]{3,2,1,0:T(8,128)} broadcast(f32[7,32]{1,0:T(8,128)S(1)} %copy.15), dimensions={0,2} | broadcast | bytes 14680960 | tf_op jit(solution)/shard_map/mul | solution.py:19
  380.1 1.1 copy-done.1
  381.2 13.7 %fusion = bf16[896,4096]{1,0:T(8,128)(2,1)S(1)} fusion(f32[896,4096]{1,0:T(8,128)S(1)} %copy-done.1, f32[112,8,32,128]{3,2,1,0:T(8,128)} %bitcast.34), kind=kLoop, calls=%fused_computation.1 | loop fusion | flops 7340032 | bytes 36700160 | tf_op jit(solution)/shard_map/convert_element_type | solution.py:20
  394.9 0.0 copy-start.2
  394.9 2.9 copy-done.2
  397.9 0.0 copy-done.3
  397.9 3.9 fusion.1
  401.7 4.2 copy.19
  405.9 0.0 reduce-scatter.4.cloned.1.call-update
  405.9 5.2 %fusion.2 = bf16[256,896]{0,1:T(8,128)(2,1)S(1)} fusion(bf16[896,4096]{1,0:T(8,128)(2,1)} %copy-done.2, bf16[256,4096]{1,0:T(8,128)(2,1)S(1)} %copy-done), kind=kOutput, calls=%fused_computation.13 | convolution fusion | flops 1879277568 | bytes 9895936 | tf_op jit(solution)/shard_map/dot_general | solution.py:33
  411.1 1.0 copy.18
  412.1 0.0 all-to-all-done
  412.1 4.9 convert_reduce_fusion
  417.0 75.4 %reduce-scatter.4.cloned.1.call-done = bf16[16,4096]{1,0:T(8,128)(2,1)} async-done(((bf16[256,4096]{1,0:T(8,128)(2,1)}), bf16[16,4096]{1,0:T(8,128)(2,1)}) %reduce-scatter.4.cloned.1.call-update) | async-done | bytes 131088
  (1 shorter events, 0.0 us)
Async XLA Ops:
  7.2 1.6 copy-start
  7.2 324.4 %all-gather.3.cloned.1.call-start = ((), (), s32[]{:S(2)}) async-start(), calls=%async_computation.2 | async-start | bytes 3784704 | tf_op jit(solution)/shard_map/all_gather | solution.py:24
  16.9 16.8 %copy-start.4 = (f32[7,1]{0,1:T(1,128)S(1)}, f32[7,1]{0,1:T(1,128)}, u32[]{:S(2)}) copy-start(f32[7,1]{0,1:T(1,128)} %param.7) | copy-start | bytes 88
  16.9 395.1 %all-to-all-start = ((bf16[896,32,128]{2,0,1:T(8,128)(2,1)}), bf16[896,32,128]{2,0,1:T(8,128)(2,1)}, u32[]{:S(2)}, u32[]{:S(2)}) async-start(bf16[896,32,128]{2,0,1:T(8,128)(2,1)} %bitcast.35), calls=%async_computation | async-start | bytes 14680064 | tf_op jit(solution)/shard_map/all_to_all | solution.py:40
  33.7 458.7 %reduce-scatter.4.cloned.1.call-start = ((), (), s32[]{:S(2)}) async-start(), calls=%async_computation.3 | async-start | bytes 2228224
  370.7 10.5 %copy-start.1 = (f32[896,4096]{1,0:T(8,128)S(1)}, f32[896,4096]{1,0:T(8,128)}, u32[]{:S(2)}) copy-start(f32[896,4096]{1,0:T(8,128)} %convert_element_type.31) | copy-start | bytes 44040196
  381.2 16.7 %copy-start.3 = (bf16[256,896]{1,0:T(8,128)(2,1)S(1)}, bf16[256,896]{1,0:T(8,128)(2,1)}, u32[]{:S(2)}) copy-start(bf16[256,896]{1,0:T(8,128)(2,1)} %param.4) | copy-start | bytes 1376260
  394.9 2.9 copy-start.2
Sparse Core Ops, SparseCore 0:
  11.1 317.6 all-gather.2
  406.1 86.2 reduce-scatter.3
where the time goes:
time: 502 us; the launch traced here: 499 us
  blocking collectives  298 us (59%)
  waiting for transfers between devices  76.1 us (15%)
  local copies, waits for them, and re-layouts  58.3 us (12%)
  other arithmetic  24.1 us (5%)
  starting transfers between devices  16.8 us (3%)
  between operations  14.1 us (3%)
  matrix products  12.2 us (2%)
    all_gather x1, blocking collectives, per_device(): all_scales = lax.all_gather(block_scales, 'intra', axis=1, tiled=True)  298 us
    unnamed x3, waiting for transfers between devices  76.1 us
    convert_element_type x2, local copies, waits for them, and re-layouts, unpack_weight(): unpacked = stacked.reshape(-1, packed_codes.shape[1]).astype(jnp.float32)  33.7 us
    all_to_all x1, starting transfers between devices, per_device(): lax.all_to_all(grad_term, 'intra', split_axis=1, concat_axis=0, tiled=True)  16.8 us
    convert_element_type x1, other arithmetic, unpack_weight(): return scaled.reshape(row_total, col_total).astype(jnp.bfloat16)  13.7 us
    unnamed x13, local copies, waits for them, and re-layouts  10.1 us
  transfers between devices with their start and end apart: 3, of which 1 were waited for; matrix products, arithmetic and copies ran while one was open for 18% of the time, Pallas kernels for 0%

commit v1 on v0

v1 whole, which is shorter than its diff:
```python
import functools

import jax
import jax.numpy as jnp
from jax import lax
from jax.experimental import pallas as pl
from jax.experimental.pallas import tpu as pltpu
from jax.sharding import Mesh, PartitionSpec as P

Z_LO, X, CORE, Z_HI, Y = 2, 4, 2, 4, 8
FINE = ("z_lo", "x", "core", "z_hi", "y")
BF16, F32 = jnp.bfloat16, jnp.float32
HALF = 112
HIDDEN_DEV = 896
SCALE_ROWS = 8
EXACT = 2.0**34


def pack_block(codes, scales):
    words = jnp.bitwise_or(codes[:HALF], jnp.left_shift(codes[HALF:], 16))
    whole = (scales * EXACT).astype(jnp.int32)
    whole = jnp.pad(whole, ((0, SCALE_ROWS - whole.shape[0]), (0, 0)))
    whole = jnp.broadcast_to(whole, (SCALE_ROWS, codes.shape[1]))
    return jnp.concatenate([words, whole], axis=0)


def unpack_into(block, wide):
    words = block[:HALF]
    scales = block[HALF:].astype(F32) * (1.0 / EXACT)
    for slot in range(8):
        level = jnp.bitwise_and(jnp.right_shift(words, 4 * slot), 15) - 8
        wide[pl.ds((slot // 4) * 4 * HALF + slot % 4, HALF, stride=4), :] = level.astype(F32)
    parts = []
    for b in range(HIDDEN_DEV // 128):
        parts.append((wide[b * 128 : (b + 1) * 128, :] * scales[b : b + 1, :]).astype(BF16))
    return parts


def near_kernel(hid_ref, blocks_ref, out_ref, wide, weight):
    @pl.when(pl.program_id(0) == 0)
    def _():
        for z in range(Z_HI):
            for b, part in enumerate(unpack_into(blocks_ref[z], wide.at[z])):
                weight[b * 128 : (b + 1) * 128, z * 128 : (z + 1) * 128] = part

    out_ref[0] = jnp.dot(hid_ref[0], weight[...], preferred_element_type=F32).astype(BF16)


def near_product(hid, blocks):
    groups, rows, depth = hid.shape
    return pl.pallas_call(
        near_kernel,
        grid=(groups,),
        in_specs=[
            pl.BlockSpec((1, rows, depth), lambda g: (g, 0, 0)),
            pl.BlockSpec(blocks.shape, lambda g: (0, 0, 0)),
        ],
        out_specs=pl.BlockSpec((1, rows, Z_HI * 128), lambda g: (g, 0, 0)),
        out_shape=jax.ShapeDtypeStruct((groups, rows, Z_HI * 128), BF16),
        scratch_shapes=[
            pltpu.VMEM((Z_HI, HIDDEN_DEV, 128), F32),
            pltpu.VMEM((HIDDEN_DEV, Z_HI * 128), BF16),
        ],
        cost_estimate=pl.CostEstimate(
            flops=2 * groups * rows * depth * Z_HI * 128, bytes_accessed=8_000_000, transcendentals=0
        ),
        compiler_params=pltpu.CompilerParams(vmem_limit_bytes=32 * 1024 * 1024),
    )(hid, blocks)


def grad_hidden_kernel(cot_ref, blocks_ref, out_ref, wide, weight, total):
    step = pl.program_id(0)
    cot = []
    for z in range(Z_HI):
        for b, part in enumerate(unpack_into(blocks_ref[0, z], wide.at[z])):
            weight[b * 128 : (b + 1) * 128, z * 128 : (z + 1) * 128] = part
        cot.append(cot_ref[:, pl.ds(pl.multiple_of(z * Y * 128 + step * 128, 128), 128)])
    term = lax.dot_general(
        jnp.concatenate(cot, axis=1), weight[...], (((1,), (1,)), ((), ())), preferred_element_type=F32
    )

    @pl.when(step == 0)
    def _():
        total[...] = term

    @pl.when(step > 0)
    def _():
        total[...] += term

    @pl.when(step == pl.num_programs(0) - 1)
    def _():
        out_ref[...] = total[...].astype(BF16)


def grad_hidden_of(cot, blocks):
    rows = cot.shape[0]
    return pl.pallas_call(
        grad_hidden_kernel,
        grid=(Y,),
        in_specs=[
            pl.BlockSpec(cot.shape, lambda g: (0, 0)),
            pl.BlockSpec((1,) + blocks.shape[1:], lambda g: (g, 0, 0, 0)),
        ],
        out_specs=pl.BlockSpec((rows, HIDDEN_DEV), lambda g: (0, 0)),
        out_shape=jax.ShapeDtypeStruct((rows, HIDDEN_DEV), BF16),
        scratch_shapes=[
            pltpu.VMEM((Z_HI, HIDDEN_DEV, 128), F32),
            pltpu.VMEM((HIDDEN_DEV, Z_HI * 128), BF16),
            pltpu.VMEM((rows, HIDDEN_DEV), F32),
        ],
        cost_estimate=pl.CostEstimate(
            flops=2 * rows * HIDDEN_DEV * cot.shape[1], bytes_accessed=6_000_000, transcendentals=0
        ),
        compiler_params=pltpu.CompilerParams(vmem_limit_bytes=32 * 1024 * 1024),
    )(cot, blocks)


def ring(size, step):
    return [(i, (i + step) % size) for i in range(size)]


def per_device(hidden, cotangent, packed_codes, block_scales):
    tokens = hidden.shape[0]
    core = lax.axis_index("core")

    block = pack_block(packed_codes, block_scales)
    near = lax.all_gather(block, "z_hi")
    hid = lax.all_gather(hidden, "y")

    cols = cotangent.reshape(tokens, 2, 2, Y, 128)
    half = lax.dynamic_index_in_dim(cols, core, 1, keepdims=False)
    half = half.transpose(2, 0, 1, 3).reshape(Y, tokens, 256)
    mine = lax.all_to_all(half, "y", 0, 0)
    other = lax.ppermute(mine, "core", ring(CORE, 1))
    first = jnp.where(core == 0, mine, other)
    second = jnp.where(core == 0, other, mine)
    cot = jnp.concatenate([first, second], axis=2)

    term = lax.dot_general(hid, cot, (((0, 1), (0, 1)), ((), ())), preferred_element_type=F32).astype(BF16)
    terms = lax.all_to_all(term, "z_hi", split_axis=1, concat_axis=0, tiled=True)
    grad_weight = jnp.sum(terms.reshape(Z_HI, HIDDEN_DEV, 128).astype(F32), axis=0)

    partial = near_product(hid, near)
    partial = partial.reshape(Y, Z_LO * X, CORE, 16, 512)
    halves = lax.all_to_all(partial, "core", split_axis=2, concat_axis=2, tiled=True)
    pair = jnp.sum(halves.astype(F32), axis=2).astype(BF16)
    pieces = lax.all_to_all(pair, ("z_lo", "x"), split_axis=1, concat_axis=1, tiled=True)
    rows = jnp.sum(pieces.astype(F32), axis=1).astype(BF16)
    rows = lax.all_to_all(rows, "y", 0, 0)
    output = rows.reshape(Y, 16, Z_HI, 128).transpose(1, 2, 0, 3).reshape(16, Z_HI * Y * 128)

    every = lax.all_gather(near, "y")
    grad_hidden = grad_hidden_of(cotangent, every)
    return output, grad_hidden, grad_weight


def solution(mesh):
    fine = Mesh(mesh.devices.reshape(Z_LO, X, CORE, Z_HI, Y), FINE)
    inter, intra = ("z_lo", "x", "core"), ("z_hi", "y")
    return jax.shard_map(
        per_device,
        mesh=fine,
        in_specs=(P(intra, inter), P(intra, None), P(inter, intra), P(inter, intra)),
        out_specs=(P(intra + inter, None), P(intra, inter), P(inter, intra)),
        check_vma=False,
    )
```

time: 502 us -> 175 us (0.35)
  the two profiles are of different devices: /device:TPU:1 before, /device:TPU:72 now
where the time goes in v1:
time: 175 us
  waiting for transfers between devices  69.5 us (40%)
  starting transfers between devices  31 us (18%)
  blocking collectives  25.5 us (15%)
  between operations  14.2 us (8%)
  local copies, waits for them, and re-layouts  13.7 us (8%)
  Pallas kernels  11.9 us (7%)
  other arithmetic  5.55 us (3%)
  matrix products  3.26 us (2%)
    all_gather x1, waiting for transfers between devices, per_device(): hid = lax.all_gather(hidden, 'y')  22.9 us
    all_to_all x1, waiting for transfers between devices, per_device(): lax.all_to_all(term, 'z_hi', split_axis=1, concat_axis=0, tiled=True)  22.8 us
    all_gather x1, blocking collectives, per_device(): near = lax.all_gather(block, 'z_hi')  20.1 us
    all_to_all x1, waiting for transfers between devices, per_device(): mine = lax.all_to_all(half, 'y', 0, 0)  14.1 us
    all_to_all x1, starting transfers between devices, per_device(): lax.all_to_all(term, 'z_hi', split_axis=1, concat_axis=0, tiled=True)  9.41 us
    unnamed x17, local copies, waits for them, and re-layouts  9.15 us
    all_to_all x1, waiting for transfers between devices, per_device(): lax.all_to_all(pair, ('z_lo', 'x'), split_axis=1, concat_axis=1, tiled=True)  8.98 us
    pallas_call x1, Pallas kernels, grad_hidden_of(): pl.pallas_call(grad_hidden_kernel, grid=(Y,), in_specs=[pl.BlockSpec(cot....  7.86 us
  transfers between devices with their start and end apart: 7, of which 4 were waited for; matrix products, arithmetic and copies ran while one was open for 9% of the time, Pallas kernels for 7%

profile of v1, /device:TPU:72, one launch (start us, length us, event | category | flops | bytes accessed | tf_op | source)
XLA Modules:
  0.0 174.6 jit_solution(7268530613157908262)
XLA Ops:
  7.2 0.7 all-gather.6.cloned.1.call-update
  7.9 2.1 %copy.21 = bf16[32,8,32,128]{3,2,1,0:T(8,128)(2,1)S(1)} copy(bf16[32,8,32,128]{3,1,2,0:T(8,128)(2,1)} %bitcast.26) | data formatting | bytes 4194304
  10.0 0.2 constant_dynamic-slice_fusion
  10.2 1.6 copy.18
  11.8 7.5 %all-to-all-start.3 = ((bf16[8,256,256]{1,2,0:T(8,128)(2,1)}), bf16[8,256,256]{1,2,0:T(8,128)(2,1)S(1)}, u32[]{:S(2)}, u32[]{:S(2)}) async-start(bf16[8,256,256]{1,2,0:T(8,128)(2,1)} %bitcast.8), calls=%async_computation.3 | async-start | bytes 2097152 | tf_op jit(solution)/shard_map/all_to_all | solution.py:133
  19.5 0.1 pad_add_fusion
  19.6 20.1 %all-gather.1 = s32[480,128]{1,0:T(8,128)} all-gather(s32[120,128]{1,0:T(8,128)S(1)} %pad_add_fusion), channel_id=3, replica_groups=mesh['z_lo'=2,'x'=4,'core'=2,'z_hi'=4,'y'=8] {'z_hi'}, dimensions={0}, use_global_device_ids=true | all-gather | bytes 307200 | tf_op jit(solution)/shard_map/all_gather | solution.py:127
  39.7 14.1 %all-to-all-done.3 = bf16[8,256,256]{1,2,0:T(8,128)(2,1)S(1)} async-done(((bf16[8,256,256]{1,2,0:T(8,128)(2,1)}), bf16[8,256,256]{1,2,0:T(8,128)(2,1)S(1)}, u32[]{:S(2)}, u32[]{:S(2)}) %all-to-all-start.3) | async-done | bytes 1048608 | tf_op jit(solution)/shard_map/all_to_all | solution.py:133
  53.8 1.9 %collective-permute-start = (bf16[8,256,256]{1,2,0:T(8,128)(2,1)S(1)}, bf16[8,256,256]{1,2,0:T(8,128)(2,1)}, u32[]{:S(2)}, u32[]{:S(2)}) collective-permute-start(bf16[8,256,256]{1,2,0:T(8,128)(2,1)S(1)} %all-to-all-done.3), channel_id=1, source_target_pairs={{0,32},{32,0},{1,33},{33,1},{2,34},{34,2},{3,35},{35,3},{4,36},{36... | collective-permute-start | bytes 3145736 | tf_op jit(solution)/shard_map/ppermute | solution.py:134
  55.7 22.9 %all-gather.6.cloned.1.call-done = bf16[2048,896]{1,0:T(8,128)(2,1)} async-done(((bf16[256,896]{1,0:T(8,128)(2,1)}), bf16[2048,896]{1,0:T(8,128)(2,1)}) %all-gather.6.cloned.1.call-update) | async-done | bytes 3670032 | tf_op jit(solution)/shard_map/all_gather | solution.py:128
  78.6 0.9 copy-done.1
  79.6 2.0 %copy-done.2 = bf16[2048,896]{1,0:T(8,128)(2,1)S(1)} copy-done((bf16[2048,896]{1,0:T(8,128)(2,1)S(1)}, bf16[2048,896]{1,0:T(8,128)(2,1)}, u32[]{:S(2)}) %copy-start.2) | copy-done | bytes 3670040
  81.6 4.1 %shard_map.67 = bf16[8,256,512]{2,1,0:T(8,128)(2,1)S(1)} custom-call(bf16[8,256,896]{2,1,0:T(8,128)(2,1)S(1)} %bitcast.30, s32[4,120,128]{2,1,0:T(8,128)S(1)} %bitcast.29), custom_call_target="tpu_custom_call" | custom-call | flops 1879048192 | bytes 8000000 | tf_op jit(solution)/shard_map/pallas_call | solution.py:51
  85.7 0.2 copy.15
  85.9 5.4 %all_to_all.33 = bf16[8,8,2,16,512]{4,3,1,0,2:T(8,128)(2,1)S(1)} all-to-all(bf16[8,8,2,16,512]{4,3,1,0,2:T(8,128)(2,1)S(1)} %copy.15), channel_id=1, replica_groups=mesh['z_lo'=2,'x'=4,'core'=2,'z_hi'=4,'y'=8] {'core'}, dimensions={2} | all-to-all | bytes 4194304 | tf_op jit(solution)/shard_map/all_to_all | solution.py:145
  91.3 1.7 reduce_sum.33
  93.0 2.3 %copy.16 = bf16[8,8,16,512]{3,2,0,1:T(8,128)(2,1)} copy(bf16[8,8,16,512]{3,2,1,0:T(8,128)(2,1)} %reduce_sum.33) | data formatting | bytes 2097152 | tf_op jit(solution)/shard_map/reduce_sum | solution.py:146
  95.3 5.8 %all-to-all-start.1 = ((bf16[8,8,16,512]{3,2,0,1:T(8,128)(2,1)}), bf16[8,8,16,512]{3,2,0,1:T(8,128)(2,1)}, u32[]{:S(2)}, u32[]{:S(2)}) async-start(bf16[8,8,16,512]{3,2,0,1:T(8,128)(2,1)} %copy.16), calls=%async_computation.1 | async-start | bytes 2097152 | tf_op jit(solution)/shard_map/all_to_all | solution.py:147
  101.1 1.5 broadcast_select_fusion.1
  102.6 0.9 copy-done.3
  103.5 3.3 %bitcast_convert_fusion = bf16[512,896]{1,0:T(8,128)(2,1)} fusion(bf16[8,256,896]{2,1,0:T(8,128)(2,1)S(1)} %bitcast.31, bf16[8,256,256]{1,2,0:T(8,128)(2,1)S(1)} %get-tuple-element.10, bf16[8,256,256]{1,2,0:T(8,128)(2,1)S(1)} %get-tuple-element.9), kind=kOutput, calls=%fused_computation.4 | convolution fusion | flops 1883701248 | bytes 6684672 | tf_op jit(solution)/shard_map/dot_general | solution.py:139
  106.7 9.0 %all-to-all-done.1 = bf16[8,8,16,512]{3,2,0,1:T(8,128)(2,1)} async-done(((bf16[8,8,16,512]{3,2,0,1:T(8,128)(2,1)}), bf16[8,8,16,512]{3,2,0,1:T(8,128)(2,1)}, u32[]{:S(2)}, u32[]{:S(2)}) %all-to-all-start.1) | async-done | bytes 1048608 | tf_op jit(solution)/shard_map/all_to_all | solution.py:147
  115.7 9.4 %all-to-all-start.4 = ((bf16[896,4,128]{0,2,1:T(8,128)(2,1)}), bf16[896,4,128]{0,2,1:T(8,128)(2,1)S(1)}, u32[]{:S(2)}, u32[]{:S(2)}) async-start(bf16[896,4,128]{0,2,1:T(8,128)(2,1)} %bitcast.34), calls=%async_computation.4 | async-start | bytes 1835008 | tf_op jit(solution)/shard_map/all_to_all | solution.py:140
  125.1 2.1 %reduce_sum.34 = bf16[8,16,512]{2,1,0:T(8,128)(2,1)} reduce(bf16[8,8,16,512]{3,2,0,1:T(8,128)(2,1)} %all-to-all-done.1, bf16[]{:T(256)} %constant.17.clone.1), dimensions={1}, to_apply=%region_1.2 | reduce | flops 458752 | bytes 1179650 | tf_op jit(solution)/shard_map/reduce_sum | solution.py:148
  127.2 22.8 %all-to-all-done.4 = bf16[896,4,128]{0,2,1:T(8,128)(2,1)S(1)} async-done(((bf16[896,4,128]{0,2,1:T(8,128)(2,1)}), bf16[896,4,128]{0,2,1:T(8,128)(2,1)S(1)}, u32[]{:S(2)}, u32[]{:S(2)}) %all-to-all-start.4) | async-done | bytes 917536 | tf_op jit(solution)/shard_map/all_to_all | solution.py:140
  150.0 6.4 %all-to-all-start.2 = ((bf16[8,16,512]{2,1,0:T(8,128)(2,1)}), bf16[8,16,512]{2,1,0:T(8,128)(2,1)S(1)}, u32[]{:S(2)}, u32[]{:S(2)}) async-start(bf16[8,16,512]{2,1,0:T(8,128)(2,1)} %reduce_sum.34), calls=%async_computation.2 | async-start | bytes 262144 | tf_op jit(solution)/shard_map/all_to_all | solution.py:149
  156.4 1.5 copy-done.4
  157.9 7.9 %shard_map.68 = bf16[256,896]{1,0:T(8,128)(2,1)} custom-call(bf16[256,4096]{1,0:T(8,128)(2,1)S(1)} %copy-done, s32[8,4,120,128]{3,2,1,0:T(8,128)S(1)} %bitcast.32), custom_call_target="tpu_custom_call" | custom-call | flops 1879048192 | bytes 6000000 | tf_op jit(solution)/shard_map/pallas_call | solution.py:97
  165.8 0.1 convert_reduce_fusion
  165.9 1.0 copy.19
  166.9 0.1 copy.17
  167.0 0.7 copy.23
  (21 shorter events, 0.2 us)
Async XLA Ops:
  7.2 71.4 %all-gather.6.cloned.1.call-start = ((), (), s32[]{:S(2)}) async-start(), calls=%async_computation.5 | async-start | bytes 4128768 | tf_op jit(solution)/shard_map/all_gather | solution.py:128
  10.2 9.2 %copy-start.6 = (f32[7,1]{0,1:T(1,128)S(1)}, f32[7,1]{0,1:T(1,128)}, u32[]{:S(2)}) copy-start(f32[7,1]{0,1:T(1,128)} %param.7) | copy-start | bytes 88
  10.2 9.3 %copy-start.5 = (s32[224,128]{1,0:T(8,128)S(1)}, s32[224,128]{1,0:T(8,128)}, u32[]{:S(2)}) copy-start(s32[224,128]{1,0:T(8,128)} %param.6) | copy-start | bytes 344068
  11.8 42.0 %all-to-all-start.3 = ((bf16[8,256,256]{1,2,0:T(8,128)(2,1)}), bf16[8,256,256]{1,2,0:T(8,128)(2,1)S(1)}, u32[]{:S(2)}, u32[]{:S(2)}) async-start(bf16[8,256,256]{1,2,0:T(8,128)(2,1)} %bitcast.8), calls=%async_computation.3 | async-start | bytes 2097152 | tf_op jit(solution)/shard_map/all_to_all | solution.py:133
  19.4 137.0 %all-gather.8.cloned.1.call-start = ((), (), s32[]{:S(2)}) async-start(), calls=%async_computation.6 | async-start | bytes 2211840 | tf_op jit(solution)/shard_map/all_gather | solution.py:152
  53.8 47.3 %collective-permute-start = (bf16[8,256,256]{1,2,0:T(8,128)(2,1)S(1)}, bf16[8,256,256]{1,2,0:T(8,128)(2,1)}, u32[]{:S(2)}, u32[]{:S(2)}) collective-permute-start(bf16[8,256,256]{1,2,0:T(8,128)(2,1)S(1)} %all-to-all-done.3), channel_id=1, source_target_pairs={{0,32},{32,0},{1,33},{33,1},{2,34},{34,2},{3,35},{35,3},{4,36},{36... | collective-permute-start | bytes 3145736 | tf_op jit(solution)/shard_map/ppermute | solution.py:134
  78.6 0.9 copy-start.1
  79.6 2.0 %copy-start.2 = (bf16[2048,896]{1,0:T(8,128)(2,1)S(1)}, bf16[2048,896]{1,0:T(8,128)(2,1)}, u32[]{:S(2)}) copy-start(bf16[2048,896]{1,0:T(8,128)(2,1)} %all-gather.6.cloned.1.call-done) | copy-start | bytes 11010052
  95.3 20.4 %all-to-all-start.1 = ((bf16[8,8,16,512]{3,2,0,1:T(8,128)(2,1)}), bf16[8,8,16,512]{3,2,0,1:T(8,128)(2,1)}, u32[]{:S(2)}, u32[]{:S(2)}) async-start(bf16[8,8,16,512]{3,2,0,1:T(8,128)(2,1)} %copy.16), calls=%async_computation.1 | async-start | bytes 2097152 | tf_op jit(solution)/shard_map/all_to_all | solution.py:147
  101.1 2.4 %copy-start.3 = (bf16[2048,896]{1,0:T(8,128)(2,1)S(1)}, bf16[2048,896]{1,0:T(8,128)(2,1)}, u32[]{:S(2)}) copy-start(bf16[2048,896]{1,0:T(8,128)(2,1)} %all-gather.6.cloned.1.call-done) | copy-start | bytes 11010052
  106.7 49.7 %copy-start = (bf16[256,4096]{1,0:T(8,128)(2,1)S(1)}, bf16[256,4096]{1,0:T(8,128)(2,1)}, u32[]{:S(2)}) copy-start(bf16[256,4096]{1,0:T(8,128)(2,1)} %cot_ref.1) | copy-start | bytes 6291460
  115.7 34.3 %all-to-all-start.4 = ((bf16[896,4,128]{0,2,1:T(8,128)(2,1)}), bf16[896,4,128]{0,2,1:T(8,128)(2,1)S(1)}, u32[]{:S(2)}, u32[]{:S(2)}) async-start(bf16[896,4,128]{0,2,1:T(8,128)(2,1)} %bitcast.34), calls=%async_computation.4 | async-start | bytes 1835008 | tf_op jit(solution)/shard_map/all_to_all | solution.py:140
  150.0 16.9 %all-to-all-start.2 = ((bf16[8,16,512]{2,1,0:T(8,128)(2,1)}), bf16[8,16,512]{2,1,0:T(8,128)(2,1)S(1)}, u32[]{:S(2)}, u32[]{:S(2)}) async-start(bf16[8,16,512]{2,1,0:T(8,128)(2,1)} %reduce_sum.34), calls=%async_computation.2 | async-start | bytes 262144 | tf_op jit(solution)/shard_map/all_to_all | solution.py:149
  156.4 1.5 copy-start.4
Sparse Core Ops, SparseCore 0:
  10.1 68.4 all-gather.5
  80.7 45.6 all-gather.7

commit v2 on v1

v2 whole, which is shorter than its diff:
```python
import functools

import jax
import jax.numpy as jnp
from jax import lax
from jax.experimental import pallas as pl
from jax.experimental.pallas import tpu as pltpu
from jax.sharding import Mesh, PartitionSpec as P

Z_LO, X, CORE, Z_HI, Y = 2, 4, 2, 4, 8
FINE = ("z_lo", "x", "core", "z_hi", "y")
BF16, F32 = jnp.bfloat16, jnp.float32
HALF = 112
HIDDEN_DEV = 896
SCALE_ROWS = 8
EXACT = 2.0**34
SIGNS = -0x77777778
VMEM_BYTES = 56 * 1024 * 1024


def pack_block(codes, scales):
    words = jnp.bitwise_or(codes[:HALF], jnp.left_shift(codes[HALF:], 16))
    words = jnp.bitwise_xor(words, SIGNS)
    whole = (scales * EXACT).astype(jnp.int32)
    whole = jnp.pad(whole, ((0, SCALE_ROWS - whole.shape[0]), (0, 0)))
    whole = jnp.broadcast_to(whole, (SCALE_ROWS, codes.shape[1]))
    return jnp.concatenate([words, whole], axis=0)


def level_of(words, slot):
    return jnp.right_shift(jnp.left_shift(words, 28 - 4 * slot), 28).astype(F32)


def scales_of(block):
    return block[HALF:].astype(F32) * (1.0 / EXACT)


def unpack_kernel(block_ref, out_ref, wide):
    block = block_ref[0]
    words, scales = block[:HALF], scales_of(block)
    for slot in range(8):
        wide[pl.ds((slot // 4) * 4 * HALF + slot % 4, HALF, stride=4), :] = level_of(words, slot)
    for b in range(HIDDEN_DEV // 128):
        rows = slice(b * 128, (b + 1) * 128)
        out_ref[rows, :] = (wide[rows, :] * scales[b : b + 1, :]).astype(BF16)


def near_weight(blocks):
    count, rows, lanes = blocks.shape
    return pl.pallas_call(
        unpack_kernel,
        grid=(count,),
        in_specs=[pl.BlockSpec((1, rows, lanes), lambda z: (z, 0, 0))],
        out_specs=pl.BlockSpec((HIDDEN_DEV, lanes), lambda z: (0, z)),
        out_shape=jax.ShapeDtypeStruct((HIDDEN_DEV, count * lanes), BF16),
        scratch_shapes=[pltpu.VMEM((HIDDEN_DEV, 128), F32)],
        cost_estimate=pl.CostEstimate(flops=2_000_000, bytes_accessed=1_200_000, transcendentals=0),
    )(blocks)


def assemble_kernel(place_ref, a_ref, b_ref, c_ref, out_ref):
    core, z_lo = place_ref[0], place_ref[1]
    for part, lo, co in (
        (a_ref, z_lo, core),
        (b_ref, 1 - z_lo, core),
        (c_ref.at[0], z_lo, 1 - core),
        (c_ref.at[1], 1 - z_lo, 1 - core),
    ):
        out_ref[:, pl.ds(pl.multiple_of((lo * 2 + co) * 64, 64), 64), :] = part[...]


def assemble(place, a, b, c):
    groups, quarter, width = a.shape
    step = 4
    part = pl.BlockSpec((step, quarter, width), lambda g, place: (g, 0, 0))
    return pl.pallas_call(
        assemble_kernel,
        grid_spec=pltpu.PrefetchScalarGridSpec(
            num_scalar_prefetch=1,
            grid=(groups // step,),
            in_specs=[part, part, pl.BlockSpec((2, step, quarter, width), lambda g, place: (0, g, 0, 0))],
            out_specs=pl.BlockSpec((step, 4 * quarter, width), lambda g, place: (g, 0, 0)),
        ),
        out_shape=jax.ShapeDtypeStruct((groups, 4 * quarter, width), BF16),
        cost_estimate=pl.CostEstimate(flops=0, bytes_accessed=4_000_000, transcendentals=0),
        compiler_params=pltpu.CompilerParams(vmem_limit_bytes=32 * 1024 * 1024),
    )(place, a, b, c)


def rows_kernel(other, place_ref, hid_ref, weight_ref, *rest):
    if other:
        out_ref, hid, weight, out, sems, out_sems = rest
        core = 1 - place_ref[0]
    else:
        got_ref, out_ref, hid, weight, out, sems, out_sems, got, got_sems = rest
        core = place_ref[0]
    chunks, groups, parts, rows, depth = hid.shape
    load = pltpu.make_async_copy(weight_ref, weight, sems.at[chunks])
    load.start()
    loads, adds, stores = [], [], []
    for i in range(chunks):
        at = pl.ds(i * groups, groups)
        loads.append(pltpu.make_async_copy(hid_ref.at[at, :, core], hid.at[i], sems.at[i]))
        loads[i].start()
        if not other:
            adds.append(pltpu.make_async_copy(got_ref.at[:, at], got.at[i], got_sems.at[i]))
            adds[i].start()
        stores.append(pltpu.make_async_copy(out.at[i], out_ref.at[:, at], out_sems.at[i]))
    load.wait()
    for i in range(chunks):
        loads[i].wait()
        product = jnp.dot(
            hid[i].reshape(groups * parts * rows, depth), weight[...], preferred_element_type=F32
        ).reshape(groups, parts, rows, weight.shape[1])
        if not other:
            adds[i].wait()
        for g in range(groups):
            value = product[g] if other else product[g] + got[i, :, g].astype(F32)
            out[i, :, g] = value.astype(BF16)
        stores[i].start()
    for store in stores:
        store.wait()


def core_rows(place, hid, weight, got=None):
    groups, chunks = hid.shape[0], 4
    step, depth = groups // chunks, hid.shape[2]
    parts, width = Z_LO * X, weight.shape[1]
    hid = hid.reshape(groups, parts, CORE, 16, depth)
    other = got is None
    args = (hid, weight) if other else (hid, weight, got)
    buffer = pltpu.VMEM((chunks, parts, step, 16, width), BF16)
    sems = pltpu.SemaphoreType.DMA((chunks,))
    return pl.pallas_call(
        functools.partial(rows_kernel, other),
        grid_spec=pltpu.PrefetchScalarGridSpec(
            num_scalar_prefetch=1,
            grid=(1,),
            in_specs=[pl.BlockSpec(memory_space=pl.ANY)] * len(args),
            out_specs=pl.BlockSpec(memory_space=pl.ANY),
            scratch_shapes=[
                pltpu.VMEM((chunks, step, parts, 16, depth), BF16),
                pltpu.VMEM(weight.shape, BF16),
                buffer,
                pltpu.SemaphoreType.DMA((chunks + 1,)),
                sems,
            ]
            + ([] if other else [buffer, sems]),
        ),
        out_shape=jax.ShapeDtypeStruct((parts, groups, 16, width), BF16),
        cost_estimate=pl.CostEstimate(
            flops=groups * 256 * HIDDEN_DEV * width, bytes_accessed=4_000_000, transcendentals=0
        ),
        compiler_params=pltpu.CompilerParams(vmem_limit_bytes=VMEM_BYTES),
    )(place, *args)


def row_widths(part):
    return ((0, 32), (1, 32), (2, 32), (3, 16)) if part == 0 else ((3, 16), (4, 32), (5, 32), (6, 32))


def grad_hidden_kernel(*refs):
    cot_refs, (blocks_ref, out_ref, weight, total, ordered) = refs[:Z_HI], refs[Z_HI:]
    step = pl.program_id(0)
    for z in range(Z_HI):
        block = blocks_ref[0, z]
        scales = scales_of(block)
        wide = [
            jnp.concatenate([jnp.broadcast_to(scales[b : b + 1], (rows, 128)) for b, rows in row_widths(part)], axis=0)
            for part in range(2)
        ]
        for slot in range(8):
            value = (level_of(block[:HALF], slot) * wide[slot // 4]).astype(BF16)
            weight[slot * HALF : (slot + 1) * HALF, z * 128 : (z + 1) * 128] = value
    cot = jnp.concatenate([ref[...] for ref in cot_refs], axis=1)
    term = lax.dot_general(weight[...], cot, (((1,), (1,)), ((), ())), preferred_element_type=F32)

    @pl.when(step == 0)
    def _():
        total[...] = term

    @pl.when(step > 0)
    def _():
        total[...] += term

    @pl.when(step == pl.num_programs(0) - 1)
    def _():
        for half in range(2):
            lanes = slice(half * 128, (half + 1) * 128)
            for slot in range(8):
                rows = pl.ds((slot // 4) * 4 * HALF + slot % 4, HALF, stride=4)
                ordered[half, rows, :] = total[slot * HALF : (slot + 1) * HALF, lanes]
            out_ref[lanes, :] = ordered[half].T.astype(BF16)


def grad_hidden_of(cot, blocks):
    rows = cot.shape[0]
    return pl.pallas_call(
        grad_hidden_kernel,
        grid=(Y,),
        in_specs=[pl.BlockSpec((rows, 128), functools.partial(lambda z, g: (0, z * Y + g), z)) for z in range(Z_HI)]
        + [pl.BlockSpec((1,) + blocks.shape[1:], lambda g: (g, 0, 0, 0))],
        out_specs=pl.BlockSpec((rows, HIDDEN_DEV), lambda g: (0, 0)),
        out_shape=jax.ShapeDtypeStruct((rows, HIDDEN_DEV), BF16),
        scratch_shapes=[
            pltpu.VMEM((HIDDEN_DEV, Z_HI * 128), BF16),
            pltpu.VMEM((HIDDEN_DEV, rows), F32),
            pltpu.VMEM((rows // 128, HIDDEN_DEV, 128), F32),
        ],
        cost_estimate=pl.CostEstimate(
            flops=2 * rows * HIDDEN_DEV * cot.shape[1], bytes_accessed=6_000_000, transcendentals=0
        ),
        compiler_params=pltpu.CompilerParams(vmem_limit_bytes=VMEM_BYTES),
    )(*([cot] * Z_HI), blocks)


def ring(size, step):
    return [(i, (i + step) % size) for i in range(size)]


def per_device(hidden, cotangent, packed_codes, block_scales):
    core, z_lo, z_hi = (lax.axis_index(name) for name in ("core", "z_lo", "z_hi"))
    place = jnp.stack([core, z_lo]).astype(jnp.int32)

    hid = lax.all_gather(hidden, "y")
    near = lax.all_gather(pack_block(packed_codes, block_scales), "z_hi")

    mine = lax.dynamic_slice_in_dim(cotangent, (z_lo * 2 + core) * 64, 64, axis=0).reshape(64, Z_HI, Y, 128)
    mine = lax.dynamic_slice_in_dim(jnp.concatenate([mine, mine], axis=1), z_hi, Z_HI, axis=1)
    mine = mine.transpose(2, 0, 1, 3).reshape(Y, 64, Z_HI * 128)
    a = lax.all_to_all(mine, "y", 0, 0)
    a, near = lax.optimization_barrier((a, near))
    b = lax.ppermute(a, "z_lo", ring(Z_LO, 1))
    weight = near_weight(near)
    c = lax.ppermute(jnp.stack([a, b]), "core", ring(CORE, 1))
    cot = assemble(place, a, b, c)

    hid, weight, cot = lax.optimization_barrier((hid, weight, cot))
    send = core_rows(place, hid, weight)
    got = lax.ppermute(send, "core", ring(CORE, 1))
    hid, cot, _ = lax.optimization_barrier((hid, cot, send))
    term = lax.dot_general(hid, cot, (((0, 1), (0, 1)), ((), ())), preferred_element_type=F32).astype(BF16)
    term = term.reshape(HIDDEN_DEV, Z_HI, 128).transpose(1, 0, 2)
    got, term = lax.optimization_barrier((got, term))
    pair = core_rows(place, hid, weight, got)
    pieces = lax.all_to_all(pair, ("z_lo", "x"), 0, 0)
    rows = jnp.sum(pieces.astype(F32), axis=0).astype(BF16)
    output = lax.all_to_all(rows, "y", 0, 0)
    output = output.reshape(Y, 16, Z_HI, 128).transpose(1, 2, 0, 3).reshape(16, Z_HI * Y * 128)

    term, pair = lax.optimization_barrier((term, pair))
    terms = [term[0]] + [lax.ppermute(term[d], "z_hi", ring(Z_HI, d)) for d in (1, 2, 3)]

    every = lax.all_gather(near, "y")
    every, rows = lax.optimization_barrier((every, rows))
    grad_hidden = grad_hidden_of(cotangent, every)
    grad_hidden, *terms = lax.optimization_barrier((grad_hidden, *terms))
    grad_weight = sum(each.astype(F32) for each in terms)
    return output, grad_hidden, grad_weight


def solution(mesh):
    fine = Mesh(mesh.devices.reshape(Z_LO, X, CORE, Z_HI, Y), FINE)
    inter, intra = ("z_lo", "x", "core"), ("z_hi", "y")
    return jax.shard_map(
        per_device,
        mesh=fine,
        in_specs=(P(intra, inter), P(intra, None), P(inter, intra), P(inter, intra)),
        out_specs=(P(intra + inter, None), P(intra, inter), P(inter, intra)),
        check_vma=False,
    )
```

time: 175 us -> 142 us (0.81)
  the two profiles are of different devices: /device:TPU:72 before, /device:TPU:1 now
where the time goes in v2:
time: 142 us; the launch traced here: 141 us
  starting transfers between devices  45.8 us (32%)
  waiting for transfers between devices  26.2 us (18%)
  Pallas kernels  22.7 us (16%)
  blocking collectives  18.3 us (13%)
  between operations  14.3 us (10%)
  local copies, waits for them, and re-layouts  8.08 us (6%)
  matrix products  3.29 us (2%)
  other arithmetic  2.2 us (2%)
    all_gather x1, blocking collectives, per_device(): near = lax.all_gather(pack_block(packed_codes, block_scales), 'z_hi')  18.3 us
    ppermute x3, starting transfers between devices, per_device(): lax.ppermute(term[d], 'z_hi', ring(Z_HI, d))  16.4 us
    pallas_call x2, Pallas kernels, core_rows(): pl.pallas_call(functools.partial(rows_kernel, other), grid_spec=pltpu.Pre...  9.64 us
    ppermute x1, waiting for transfers between devices, per_device(): b = lax.ppermute(a, 'z_lo', ring(Z_LO, 1))  9.1 us
    pallas_call x1, Pallas kernels, grad_hidden_of(): pl.pallas_call(grad_hidden_kernel, grid=(Y,), in_specs=[pl.BlockSpec((row...  8.94 us
    ppermute x3, waiting for transfers between devices, per_device(): lax.ppermute(term[d], 'z_hi', ring(Z_HI, d))  8.7 us
    all_to_all x1, starting transfers between devices, per_device(): a = lax.all_to_all(mine, 'y', 0, 0)  7.65 us
    all_gather x1, waiting for transfers between devices, per_device(): hid = lax.all_gather(hidden, 'y')  7.52 us
  transfers between devices with their start and end apart: 11, of which 4 were waited for; matrix products, arithmetic and copies ran while one was open for 7% of the time, Pallas kernels for 16%

profile of v2, /device:TPU:1, one launch (start us, length us, event | category | flops | bytes accessed | tf_op | source)
XLA Modules:
  0.0 140.8 jit_solution(13893455569464061106)
XLA Ops:
  7.2 0.7 all-gather.6.cloned.1.call-update
  7.9 1.1 dynamic-slice_bitcast_fusion
  9.1 0.2 fusion.1
  9.3 0.2 copy.16
  9.5 1.0 reshape.28
  10.5 7.7 %all-to-all-start = ((bf16[8,64,512]{2,1,0:T(8,128)(2,1)}), bf16[8,64,512]{2,1,0:T(8,128)(2,1)S(1)}, u32[]{:S(2)}, u32[]{:S(2)}) async-start(bf16[8,64,512]{2,1,0:T(8,128)(2,1)} %reshape.28), calls=%async_computation | async-start | bytes 1048576 | tf_op jit(solution)/shard_map/all_to_all | solution.py:231
  18.4 18.3 %all-gather.1 = s32[480,128]{1,0:T(8,128)} all-gather(s32[120,128]{1,0:T(8,128)S(1)} %pad_add_fusion), channel_id=3, replica_groups=mesh['z_lo'=2,'x'=4,'core'=2,'z_hi'=4,'y'=8] {'z_hi'}, dimensions={0}, use_global_device_ids=true | all-gather | bytes 307200 | tf_op jit(solution)/shard_map/all_gather | solution.py:226
  36.7 3.9 %collective-permute-start = (bf16[8,64,512]{2,1,0:T(8,128)(2,1)S(1)}, bf16[8,64,512]{2,1,0:T(8,128)(2,1)S(1)}, u32[]{:S(2)}, u32[]{:S(2)}) collective-permute-start(bf16[8,64,512]{2,1,0:T(8,128)(2,1)S(1)} %all-to-all-done.a_ref), channel_id=1, source_target_pairs={{0,256},{256,0},{1,257},{257,1},{2,258},{258,2},{3,259},{259,3},{4... | collective-permute-start | bytes 1572872 | tf_op jit(solution)/shard_map/ppermute | solution.py:233
  40.6 9.1 %collective-permute-done.b_ref = bf16[8,64,512]{2,1,0:T(8,128)(2,1)S(1)} collective-permute-done((bf16[8,64,512]{2,1,0:T(8,128)(2,1)S(1)}, bf16[8,64,512]{2,1,0:T(8,128)(2,1)S(1)}, u32[]{:S(2)}, u32[]{:S(2)}) %collective-permute-start) | collective-permute-done | bytes 524320 | tf_op jit(solution)/shard_map/ppermute | solution.py:233
  49.8 5.7 %collective-permute-start.1 = (bf16[2,8,64,512]{3,2,1,0:T(8,128)(2,1)S(1)}, bf16[2,8,64,512]{3,2,1,0:T(8,128)(2,1)S(1)}, u32[]{:S(2)}, u32[]{:S(2)}) collective-permute-start(bf16[2,8,64,512]{3,2,1,0:T(8,128)(2,1)S(1)} %pad_maximum_fusion), channel_id=1, source_target_pairs={{0,32},{32,0},{1,33},{33,1},{2,34},{34,2},{3,35},{35,3},{4,36},{36... | collective-permute-start | bytes 3145736 | tf_op jit(solution)/shard_map/ppermute | solution.py:235
  55.6 3.3 %shard_map.67.weight_ref = bf16[896,512]{1,0:T(8,128)(2,1)} custom-call(s32[4,120,128]{2,1,0:T(8,128)} %bitcast.44), custom_call_target="tpu_custom_call" | custom-call | flops 2000000 | bytes 1200000 | tf_op jit(solution)/shard_map/pallas_call | solution.py:50
  58.9 1.0 copy-done
  59.9 1.2 copy-done.1
  61.1 0.8 shard_map.68
  61.9 7.5 %all-gather.6.cloned.1.call-done = bf16[2048,896]{1,0:T(8,128)(2,1)} async-done(((bf16[256,896]{1,0:T(8,128)(2,1)}), bf16[2048,896]{1,0:T(8,128)(2,1)}) %all-gather.6.cloned.1.call-update) | async-done | bytes 3670032 | tf_op jit(solution)/shard_map/all_gather | solution.py:225
  69.5 4.9 %shard_map.69 = bf16[8,8,16,512]{3,2,1,0:T(8,128)(2,1)} custom-call(s32[2]{0:T(128)} %copy-done.2, bf16[8,8,2,16,896]{4,3,2,1,0:T(8,128)(2,1)} %bitcast.39, bf16[896,512]{1,0:T(8,128)(2,1)} %shard_map.67.weight_ref), custom_call_target="tpu_custom_call" | custom-call | flops 939524096 | bytes 4000000 | tf_op jit(solution)/shard_map/pallas_call | solution.py:134
  74.4 2.4 %collective-permute-start.2 = (bf16[8,8,16,512]{3,2,1,0:T(8,128)(2,1)}, bf16[8,8,16,512]{3,2,1,0:T(8,128)(2,1)S(1)}, u32[]{:S(2)}, u32[]{:S(2)}) collective-permute-start(bf16[8,8,16,512]{3,2,1,0:T(8,128)(2,1)} %shard_map.69), channel_id=1, source_target_pairs={{0,32},{32,0},{1,33},{33,1},{2,34},{34,2},{3,35},{35,3},{4,36},{36... | collective-permute-start | bytes 3145736 | tf_op jit(solution)/shard_map/ppermute | solution.py:240
  76.8 3.3 %bitcast_convert_fusion = bf16[896,512]{0,1:T(8,128)(2,1)} fusion(bf16[8,256,896]{2,1,0:T(8,128)(2,1)S(1)} %bitcast.41, bf16[8,256,512]{2,1,0:T(8,128)(2,1)S(1)} %shard_map.68), kind=kOutput, calls=%fused_computation | convolution fusion | flops 1879506944 | bytes 6684672 | tf_op jit(solution)/shard_map/dot_general | solution.py:242
  80.1 1.5 %copy.18 = bf16[896,4,128]{2,0,1:T(8,128)(2,1)S(1)} copy(bf16[896,4,128]{0,2,1:T(8,128)(2,1)} %bitcast.47) | data formatting | bytes 1835008 | tf_op jit(solution)/shard_map/reshape | solution.py:243
  81.7 1.0 copy-done.4
  82.6 4.7 %shard_map.70 = bf16[8,8,16,512]{3,2,1,0:T(8,128)(2,1)} custom-call(s32[2]{0:T(128)} %copy-done.2, bf16[8,8,2,16,896]{4,3,2,1,0:T(8,128)(2,1)} %bitcast.40, bf16[896,512]{1,0:T(8,128)(2,1)} %shard_map.67.weight_ref, bf16[8,8,16,512]{3,2,1,0:T(8,128)(2,1)} %copy-done.4), custom_call_target="tpu_custom_call" | custom-call | flops 939524096 | bytes 4000000 | tf_op jit(solution)/shard_map/pallas_call | solution.py:134
  87.3 5.7 %all-to-all-start.1 = ((bf16[8,8,16,512]{3,2,1,0:T(8,128)(2,1)}), bf16[8,8,16,512]{3,2,1,0:T(8,128)(2,1)S(1)}, u32[]{:S(2)}, u32[]{:S(2)}) async-start(bf16[8,8,16,512]{3,2,1,0:T(8,128)(2,1)} %shard_map.70), calls=%async_computation.1 | async-start | bytes 2097152 | tf_op jit(solution)/shard_map/all_to_all | solution.py:246
  93.1 5.0 %collective-permute-start.3 = (bf16[896,128]{1,0:T(8,128)(2,1)S(1)}, bf16[896,128]{1,0:T(8,128)(2,1)S(1)}, u32[]{:S(2)}, u32[]{:S(2)}) collective-permute-start(bf16[896,128]{1,0:T(8,128)(2,1)S(1)} %get-tuple-element.37), channel_id=1, source_target_pairs={{0,8},{8,16},{16,24},{24,0},{1,9},{9,17},{17,25},{25,1},{2,10},{10... | collective-permute-start | bytes 688136 | tf_op jit(solution)/shard_map/ppermute | solution.py:252
  98.1 7.9 %collective-permute-start.4 = (bf16[896,128]{1,0:T(8,128)(2,1)S(1)}, bf16[896,128]{1,0:T(8,128)(2,1)S(1)}, u32[]{:S(2)}, u32[]{:S(2)}) collective-permute-start(bf16[896,128]{1,0:T(8,128)(2,1)S(1)} %get-tuple-element.36), channel_id=1, source_target_pairs={{0,16},{8,24},{16,0},{24,8},{1,17},{9,25},{17,1},{25,9},{2,18},{10... | collective-permute-start | bytes 688136 | tf_op jit(solution)/shard_map/ppermute | solution.py:252
  106.1 3.5 %collective-permute-start.5 = (bf16[896,128]{1,0:T(8,128)(2,1)S(1)}, bf16[896,128]{1,0:T(8,128)(2,1)S(1)}, u32[]{:S(2)}, u32[]{:S(2)}) collective-permute-start(bf16[896,128]{1,0:T(8,128)(2,1)S(1)} %get-tuple-element.35), channel_id=1, source_target_pairs={{0,24},{8,0},{16,8},{24,16},{1,25},{9,1},{17,9},{25,17},{2,26},{10... | collective-permute-start | bytes 688136 | tf_op jit(solution)/shard_map/ppermute | solution.py:252
  109.5 0.2 all-to-all-done.1
  109.7 0.8 reduce_sum.12
  110.5 4.0 %all-to-all-start.2 = ((bf16[8,16,512]{2,1,0:T(8,128)(2,1)}), bf16[8,16,512]{2,1,0:T(8,128)(2,1)S(1)}, u32[]{:S(2)}, u32[]{:S(2)}) async-start(bf16[8,16,512]{2,1,0:T(8,128)(2,1)} %reduce_sum.12), calls=%async_computation.2 | async-start | bytes 262144 | tf_op jit(solution)/shard_map/all_to_all | solution.py:248
  114.6 8.9 %shard_map.71 = bf16[256,896]{1,0:T(8,128)(2,1)} custom-call(bf16[256,4096]{1,0:T(8,128)(2,1)} %refs_3_.1, bf16[256,4096]{1,0:T(8,128)(2,1)} %refs_3_.1, bf16[256,4096]{1,0:T(8,128)(2,1)} %refs_3_.1, bf16[256,4096]{1,0:T(8,128)(2,1)} %refs_3_.1, s32[8,4,120,128]{3,2,1,0:T(8,128)} %bitcast.46), custom_call_target="tpu_custom_call" | custom-call | flops 1879048192 | bytes 6000000 | tf_op jit(solution)/shard_map/pallas_call | solution.py:198
  123.5 8.7 %collective-permute-done.4 = bf16[896,128]{1,0:T(8,128)(2,1)S(1)} collective-permute-done((bf16[896,128]{1,0:T(8,128)(2,1)S(1)}, bf16[896,128]{1,0:T(8,128)(2,1)S(1)}, u32[]{:S(2)}, u32[]{:S(2)}) %collective-permute-start.4) | collective-permute-done | bytes 229408 | tf_op jit(solution)/shard_map/ppermute | solution.py:252
  132.2 0.9 convert_add_fusion
  133.2 0.7 copy.24
  (32 shorter events, 0.8 us)
Async XLA Ops:
  7.2 62.3 %all-gather.6.cloned.1.call-start = ((), (), s32[]{:S(2)}) async-start(), calls=%async_computation.3 | async-start | bytes 4128768 | tf_op jit(solution)/shard_map/all_gather | solution.py:225
  9.1 9.1 %copy-start.6 = (f32[7,1]{0,1:T(1,128)S(1)}, f32[7,1]{0,1:T(1,128)}, u32[]{:S(2)}) copy-start(f32[7,1]{0,1:T(1,128)} %param.7) | copy-start | bytes 88
  9.1 9.2 %copy-start.5 = (s32[224,128]{1,0:T(8,128)S(1)}, s32[224,128]{1,0:T(8,128)}, u32[]{:S(2)}) copy-start(s32[224,128]{1,0:T(8,128)} %param.6) | copy-start | bytes 344068
  10.5 26.2 %all-to-all-start = ((bf16[8,64,512]{2,1,0:T(8,128)(2,1)}), bf16[8,64,512]{2,1,0:T(8,128)(2,1)S(1)}, u32[]{:S(2)}, u32[]{:S(2)}) async-start(bf16[8,64,512]{2,1,0:T(8,128)(2,1)} %reshape.28), calls=%async_computation | async-start | bytes 1048576 | tf_op jit(solution)/shard_map/all_to_all | solution.py:231
  18.2 96.4 %all-gather.8.cloned.1.call-start = ((), (), s32[]{:S(2)}) async-start(), calls=%async_computation.4 | async-start | bytes 2211840 | tf_op jit(solution)/shard_map/all_gather | solution.py:254
  36.7 13.0 %collective-permute-start = (bf16[8,64,512]{2,1,0:T(8,128)(2,1)S(1)}, bf16[8,64,512]{2,1,0:T(8,128)(2,1)S(1)}, u32[]{:S(2)}, u32[]{:S(2)}) collective-permute-start(bf16[8,64,512]{2,1,0:T(8,128)(2,1)S(1)} %all-to-all-done.a_ref), channel_id=1, source_target_pairs={{0,256},{256,0},{1,257},{257,1},{2,258},{258,2},{3,259},{259,3},{4... | collective-permute-start | bytes 1572872 | tf_op jit(solution)/shard_map/ppermute | solution.py:233
  49.8 9.1 %collective-permute-start.1 = (bf16[2,8,64,512]{3,2,1,0:T(8,128)(2,1)S(1)}, bf16[2,8,64,512]{3,2,1,0:T(8,128)(2,1)S(1)}, u32[]{:S(2)}, u32[]{:S(2)}) collective-permute-start(bf16[2,8,64,512]{3,2,1,0:T(8,128)(2,1)S(1)} %pad_maximum_fusion), channel_id=1, source_target_pairs={{0,32},{32,0},{1,33},{33,1},{2,34},{34,2},{3,35},{35,3},{4,36},{36... | collective-permute-start | bytes 3145736 | tf_op jit(solution)/shard_map/ppermute | solution.py:235
  55.6 6.3 %copy-start.2 = (s32[2]{0:T(128)}, s32[2]{0:T(128)S(1)}, u32[]{:S(2)}) copy-start(s32[2]{0:T(128)S(1)} %pad_add_fusion.1.place_ref) | copy-start | bytes 28
  58.9 1.0 copy-start
  59.9 1.2 copy-start.1
  69.5 7.3 %copy-start.3 = (bf16[2048,896]{1,0:T(8,128)(2,1)S(1)}, bf16[2048,896]{1,0:T(8,128)(2,1)}, u32[]{:S(2)}) copy-start(bf16[2048,896]{1,0:T(8,128)(2,1)} %all-gather.6.cloned.1.call-done) | copy-start | bytes 11010052
  74.4 7.2 %collective-permute-start.2 = (bf16[8,8,16,512]{3,2,1,0:T(8,128)(2,1)}, bf16[8,8,16,512]{3,2,1,0:T(8,128)(2,1)S(1)}, u32[]{:S(2)}, u32[]{:S(2)}) collective-permute-start(bf16[8,8,16,512]{3,2,1,0:T(8,128)(2,1)} %shard_map.69), channel_id=1, source_target_pairs={{0,32},{32,0},{1,33},{33,1},{2,34},{34,2},{3,35},{35,3},{4,36},{36... | collective-permute-start | bytes 3145736 | tf_op jit(solution)/shard_map/ppermute | solution.py:240
  81.6 1.0 copy-start.4
  87.3 22.4 %all-to-all-start.1 = ((bf16[8,8,16,512]{3,2,1,0:T(8,128)(2,1)}), bf16[8,8,16,512]{3,2,1,0:T(8,128)(2,1)S(1)}, u32[]{:S(2)}, u32[]{:S(2)}) async-start(bf16[8,8,16,512]{3,2,1,0:T(8,128)(2,1)} %shard_map.70), calls=%async_computation.1 | async-start | bytes 2097152 | tf_op jit(solution)/shard_map/all_to_all | solution.py:246
  93.1 30.4 %collective-permute-start.3 = (bf16[896,128]{1,0:T(8,128)(2,1)S(1)}, bf16[896,128]{1,0:T(8,128)(2,1)S(1)}, u32[]{:S(2)}, u32[]{:S(2)}) collective-permute-start(bf16[896,128]{1,0:T(8,128)(2,1)S(1)} %get-tuple-element.37), channel_id=1, source_target_pairs={{0,8},{8,16},{16,24},{24,0},{1,9},{9,17},{17,25},{25,1},{2,10},{10... | collective-permute-start | bytes 688136 | tf_op jit(solution)/shard_map/ppermute | solution.py:252
  98.1 34.1 %collective-permute-start.4 = (bf16[896,128]{1,0:T(8,128)(2,1)S(1)}, bf16[896,128]{1,0:T(8,128)(2,1)S(1)}, u32[]{:S(2)}, u32[]{:S(2)}) collective-permute-start(bf16[896,128]{1,0:T(8,128)(2,1)S(1)} %get-tuple-element.36), channel_id=1, source_target_pairs={{0,16},{8,24},{16,0},{24,8},{1,17},{9,25},{17,1},{25,9},{2,18},{10... | collective-permute-start | bytes 688136 | tf_op jit(solution)/shard_map/ppermute | solution.py:252
  106.1 26.2 %collective-permute-start.5 = (bf16[896,128]{1,0:T(8,128)(2,1)S(1)}, bf16[896,128]{1,0:T(8,128)(2,1)S(1)}, u32[]{:S(2)}, u32[]{:S(2)}) collective-permute-start(bf16[896,128]{1,0:T(8,128)(2,1)S(1)} %get-tuple-element.35), channel_id=1, source_target_pairs={{0,24},{8,0},{16,8},{24,16},{1,25},{9,1},{17,9},{25,17},{2,26},{10... | collective-permute-start | bytes 688136 | tf_op jit(solution)/shard_map/ppermute | solution.py:252
  110.5 22.6 %all-to-all-start.2 = ((bf16[8,16,512]{2,1,0:T(8,128)(2,1)}), bf16[8,16,512]{2,1,0:T(8,128)(2,1)S(1)}, u32[]{:S(2)}, u32[]{:S(2)}) async-start(bf16[8,16,512]{2,1,0:T(8,128)(2,1)} %reduce_sum.12), calls=%async_computation.2 | async-start | bytes 262144 | tf_op jit(solution)/shard_map/all_to_all | solution.py:248
Sparse Core Ops, SparseCore 0:
  10.1 59.3 all-gather.5
  71.5 40.5 all-gather.7

commit v3 on v2

v3 whole, which is shorter than its diff:
```python
import functools

import jax
import jax.numpy as jnp
from jax import lax
from jax.experimental import pallas as pl
from jax.experimental.pallas import tpu as pltpu
from jax.sharding import Mesh, PartitionSpec as P

Z_LO, X, CORE, Z_HI, Y = 2, 4, 2, 4, 8
FINE = ("z_lo", "x", "core", "z_hi", "y")
BF16, F32 = jnp.bfloat16, jnp.float32
HALF = 112
HIDDEN_DEV = 896
SCALE_ROWS = 8
CHUNKS = 4
SHARE = 32
EXACT = 2.0**34
SIGNS = -0x77777778
VMEM_BYTES = 56 * 1024 * 1024


def pack_block(codes, scales):
    words = jnp.bitwise_or(codes[:HALF], jnp.left_shift(codes[HALF:], 16))
    words = jnp.bitwise_xor(words, SIGNS)
    whole = (scales * EXACT).astype(jnp.int32)
    whole = jnp.pad(whole, ((0, SCALE_ROWS - whole.shape[0]), (0, 0)))
    whole = jnp.broadcast_to(whole, (SCALE_ROWS, codes.shape[1]))
    return jnp.concatenate([words, whole], axis=0)


def level_of(words, slot):
    return jnp.right_shift(jnp.left_shift(words, 28 - 4 * slot), 28).astype(F32)


def scales_of(block):
    return block[HALF:].astype(F32) * (1.0 / EXACT)


def unpack_kernel(block_ref, out_ref, wide):
    block = block_ref[0]
    words, scales = block[:HALF], scales_of(block)
    for slot in range(8):
        wide[pl.ds((slot // 4) * 4 * HALF + slot % 4, HALF, stride=4), :] = level_of(words, slot)
    for b in range(HIDDEN_DEV // 128):
        rows = slice(b * 128, (b + 1) * 128)
        out_ref[rows, :] = (wide[rows, :] * scales[b : b + 1, :]).astype(BF16)


def near_weight(blocks):
    count, rows, lanes = blocks.shape
    return pl.pallas_call(
        unpack_kernel,
        grid=(count,),
        in_specs=[pl.BlockSpec((1, rows, lanes), lambda z: (z, 0, 0))],
        out_specs=pl.BlockSpec((HIDDEN_DEV, lanes), lambda z: (0, z)),
        out_shape=jax.ShapeDtypeStruct((HIDDEN_DEV, count * lanes), BF16),
        scratch_shapes=[pltpu.VMEM((HIDDEN_DEV, 128), F32)],
        cost_estimate=pl.CostEstimate(flops=2_000_000, bytes_accessed=1_200_000, transcendentals=0),
    )(blocks)


def assemble_kernel(place_ref, *refs):
    parts, other_ref, out_ref = refs[:4], refs[4], refs[5]
    core, z_lo, x_low, z_hi = place_ref[0], place_ref[1], place_ref[2], place_ref[3]
    order = [lax.rem(z_hi + d, Z_HI) for d in range(Z_HI)]
    for i in range(4):
        lo = z_lo if i % 2 == 0 else 1 - z_lo
        x = x_low if i // 2 == 0 else 1 - x_low
        for part, co in ((parts[i], core), (other_ref.at[i], 1 - core)):
            rows = pl.ds(pl.multiple_of(((lo * 2 + x) * 2 + co) * SHARE, SHARE), SHARE)
            for j, z in enumerate(order):
                out_ref[:, rows, j * 128 : (j + 1) * 128] = part[:, :, pl.ds(pl.multiple_of(z * 128, 128), 128)]


def assemble(place, parts, other):
    groups, share, width = parts[0].shape
    step = 4
    part = pl.BlockSpec((step, share, width), lambda g, place: (g, 0, 0))
    return pl.pallas_call(
        assemble_kernel,
        grid_spec=pltpu.PrefetchScalarGridSpec(
            num_scalar_prefetch=1,
            grid=(groups // step,),
            in_specs=[part] * 4 + [pl.BlockSpec((4, step, share, width), lambda g, place: (0, g, 0, 0))],
            out_specs=pl.BlockSpec((step, 8 * share, width), lambda g, place: (g, 0, 0)),
        ),
        out_shape=jax.ShapeDtypeStruct((groups, 8 * share, width), BF16),
        cost_estimate=pl.CostEstimate(flops=0, bytes_accessed=4_000_000, transcendentals=0),
        compiler_params=pltpu.CompilerParams(vmem_limit_bytes=32 * 1024 * 1024),
    )(place, *parts, other)


def products_kernel(
    place_ref, hid_ref, weight_ref, cot_ref, keep_ref, send_ref, own_ref, up_ref, far_ref, down_ref,
    hid, weight, cot, keep, send, sems, out_sems,
):
    core = place_ref[0]
    chunks = CHUNKS
    groups, rows, depth = hid.shape
    step, width = groups // chunks, weight.shape[1]
    load_weight = pltpu.make_async_copy(weight_ref, weight, sems.at[chunks])
    load_cot = pltpu.make_async_copy(cot_ref, cot, sems.at[chunks + 1])
    loads = [
        pltpu.make_async_copy(hid_ref.at[pl.ds(i * step, step)], hid.at[pl.ds(i * step, step)], sems.at[i])
        for i in range(chunks)
    ]
    load_weight.start()
    for load in loads:
        load.start()
    load_cot.start()
    load_weight.wait()
    for i in range(chunks):
        loads[i].wait()
        product = jnp.dot(
            hid[i * step : (i + 1) * step].reshape(step * rows, depth), weight[...], preferred_element_type=F32
        )
        product = product.astype(BF16).reshape(step, Z_LO * X, CORE, 16, width)
        for g in range(step):
            first, second = product[g, :, 0], product[g, :, 1]
            keep[:, i * step + g] = jnp.where(core == 0, first, second)
            send[:, i * step + g] = jnp.where(core == 0, second, first)
    stores = [
        pltpu.make_async_copy(send, send_ref, out_sems.at[0]),
        pltpu.make_async_copy(keep, keep_ref, out_sems.at[1]),
    ]
    for store in stores:
        store.start()
    load_cot.wait()
    tokens = hid[...].reshape(groups * rows, depth)
    columns = cot[...].reshape(groups * rows, width)

    def term(i):
        part = columns[:, i * 128 : (i + 1) * 128]
        return lax.dot_general(part, tokens, (((0,), (0,)), ((), ())), preferred_element_type=F32)

    for i, ref in enumerate((own_ref, up_ref, far_ref, down_ref)):
        ref[...] = term(i).astype(ref.dtype)
    for store in stores:
        store.wait()


def products(place, hid, weight, cot):
    groups, _, depth = hid.shape
    width = weight.shape[1]
    part = (Z_LO * X, groups, 16, width)
    anywhere, vmem = pl.BlockSpec(memory_space=pl.ANY), pl.BlockSpec(memory_space=pltpu.VMEM)
    return pl.pallas_call(
        products_kernel,
        grid_spec=pltpu.PrefetchScalarGridSpec(
            num_scalar_prefetch=1,
            grid=(1,),
            in_specs=[anywhere] * 3,
            out_specs=[anywhere] * 2 + [vmem] * 4,
            scratch_shapes=[
                pltpu.VMEM(hid.shape, BF16),
                pltpu.VMEM(weight.shape, BF16),
                pltpu.VMEM(cot.shape, BF16),
                pltpu.VMEM(part, BF16),
                pltpu.VMEM(part, BF16),
                pltpu.SemaphoreType.DMA((CHUNKS + 2,)),
                pltpu.SemaphoreType.DMA((2,)),
            ],
        ),
        out_shape=[jax.ShapeDtypeStruct(part, BF16)] * 2
        + [jax.ShapeDtypeStruct((128, depth), F32)]
        + [jax.ShapeDtypeStruct((128, depth), BF16)] * 3,
        cost_estimate=pl.CostEstimate(
            flops=4 * groups * 256 * depth * width, bytes_accessed=10_000_000, transcendentals=0
        ),
        compiler_params=pltpu.CompilerParams(vmem_limit_bytes=VMEM_BYTES),
    )(place, hid, weight, cot)


def row_widths(part):
    return ((0, 32), (1, 32), (2, 32), (3, 16)) if part == 0 else ((3, 16), (4, 32), (5, 32), (6, 32))


def grad_hidden_kernel(cot_ref, blocks_ref, out_ref, cot, blocks, even, odd, total, ordered, sems):
    step = Y // CHUNKS
    load_cot = pltpu.make_async_copy(cot_ref, cot, sems.at[CHUNKS])
    loads = [
        pltpu.make_async_copy(blocks_ref.at[pl.ds(i * step, step)], blocks.at[pl.ds(i * step, step)], sems.at[i])
        for i in range(CHUNKS)
    ]
    loads[0].start()
    load_cot.start()
    for load in loads[1:]:
        load.start()
    for y in range(Y):
        if y % step == 0:
            loads[y // step].wait()
        if y == 0:
            load_cot.wait()
        weight = odd if y % 2 else even
        for z in range(Z_HI):
            block = blocks[y, z]
            scales = scales_of(block)
            wide = [
                jnp.concatenate(
                    [jnp.broadcast_to(scales[b : b + 1], (rows, 128)) for b, rows in row_widths(part)], axis=0
                )
                for part in range(2)
            ]
            for slot in range(8):
                value = (level_of(block[:HALF], slot) * wide[slot // 4]).astype(BF16)
                weight[slot * HALF : (slot + 1) * HALF, z * 128 : (z + 1) * 128] = value
        columns = [cot[:, (z * Y + y) * 128 : (z * Y + y + 1) * 128] for z in range(Z_HI)]
        term = lax.dot_general(
            weight[...], jnp.concatenate(columns, axis=1), (((1,), (1,)), ((), ())), preferred_element_type=F32
        )
        if y == 0:
            total[...] = term
        else:
            total[...] += term
    for half in range(2):
        lanes = slice(half * 128, (half + 1) * 128)
        for slot in range(8):
            rows = pl.ds((slot // 4) * 4 * HALF + slot % 4, HALF, stride=4)
            ordered[half, rows, :] = total[slot * HALF : (slot + 1) * HALF, lanes]
        out_ref[lanes, :] = ordered[half].T.astype(BF16)


def grad_hidden_of(cot, blocks):
    rows = cot.shape[0]
    return pl.pallas_call(
        grad_hidden_kernel,
        in_specs=[pl.BlockSpec(memory_space=pl.ANY)] * 2,
        out_specs=pl.BlockSpec(memory_space=pltpu.VMEM),
        out_shape=jax.ShapeDtypeStruct((rows, HIDDEN_DEV), BF16),
        scratch_shapes=[
            pltpu.VMEM(cot.shape, BF16),
            pltpu.VMEM(blocks.shape, jnp.int32),
            pltpu.VMEM((HIDDEN_DEV, Z_HI * 128), BF16),
            pltpu.VMEM((HIDDEN_DEV, Z_HI * 128), BF16),
            pltpu.VMEM((HIDDEN_DEV, rows), F32),
            pltpu.VMEM((rows // 128, HIDDEN_DEV, 128), F32),
            pltpu.SemaphoreType.DMA((CHUNKS + 1,)),
        ],
        cost_estimate=pl.CostEstimate(
            flops=2 * rows * HIDDEN_DEV * cot.shape[1], bytes_accessed=6_000_000, transcendentals=0
        ),
        compiler_params=pltpu.CompilerParams(vmem_limit_bytes=VMEM_BYTES),
    )(cot, blocks)


def ring(size, step):
    return [(i, (i + step) % size) for i in range(size)]


def per_device(hidden, cotangent, packed_codes, block_scales):
    core, z_lo, x, z_hi = (lax.axis_index(name) for name in ("core", "z_lo", "x", "z_hi"))
    place = jnp.stack([core, z_lo, x % 2, z_hi]).astype(jnp.int32)

    hid = lax.all_gather(hidden, "y")
    near = lax.all_gather(pack_block(packed_codes, block_scales), "z_hi")

    first = ((z_lo * 2 + x % 2) * 2 + core) * SHARE
    mine = lax.dynamic_slice_in_dim(cotangent, first, SHARE, axis=0)
    mine = mine.reshape(SHARE, Z_HI, Y, 128).transpose(2, 0, 1, 3).reshape(Y, SHARE, Z_HI * 128)
    mine = lax.all_to_all(mine, "y", 0, 0)
    mine, near = lax.optimization_barrier((mine, near))
    parts = [mine]
    for flip_z, flip_x in ((1, 0), (0, 1), (1, 1)):
        pairs = [(z * X + i, (z ^ flip_z) * X + (i ^ flip_x)) for z in range(Z_LO) for i in range(X)]
        parts.append(lax.ppermute(mine, ("z_lo", "x"), pairs))
    weight = near_weight(near)
    other = lax.ppermute(jnp.stack(parts), "core", ring(CORE, 1))
    cot = assemble(place, parts, other)
    hid, weight, cot = lax.optimization_barrier((hid, weight, cot))
    keep, send, own, *others = products(place, hid, weight, cot)

    got = lax.ppermute(send, "core", ring(CORE, 1))
    pair = (keep.astype(F32) + got.astype(F32)).astype(BF16)

    pair, *others = lax.optimization_barrier((pair, *others))
    terms = [lax.ppermute(others[d - 1], "z_hi", ring(Z_HI, d)) for d in (2, 1, 3)]

    pieces = lax.all_to_all(pair, ("z_lo", "x"), 0, 0)
    rows = jnp.sum(pieces.astype(F32), axis=0).astype(BF16)
    output = lax.all_to_all(rows, "y", 0, 0)
    output = output.reshape(Y, 16, Z_HI, 128).transpose(1, 2, 0, 3).reshape(16, Z_HI * Y * 128)

    every = lax.all_gather(near, "y")
    every, rows = lax.optimization_barrier((every, rows))
    grad_hidden = grad_hidden_of(cotangent, every)
    grad_hidden, *terms = lax.optimization_barrier((grad_hidden, *terms))
    grad_weight = (own + sum(term.astype(F32) for term in terms)).T
    return output, grad_hidden, grad_weight


def solution(mesh):
    fine = Mesh(mesh.devices.reshape(Z_LO, X, CORE, Z_HI, Y), FINE)
    inter, intra = ("z_lo", "x", "core"), ("z_hi", "y")
    return jax.shard_map(
        per_device,
        mesh=fine,
        in_specs=(P(intra, inter), P(intra, None), P(inter, intra), P(inter, intra)),
        out_specs=(P(intra + inter, None), P(intra, inter), P(inter, intra)),
        check_vma=False,
    )
```

time: 142 us -> 134 us (0.944)
  matrix products: 3.29 us -> 0 us
  local copies, waits for them, and re-layouts: 8.08 us -> 5.17 us
  Pallas kernels: 22.7 us -> 19.9 us
  waiting for transfers between devices: 26.2 us -> 23.5 us
  starting transfers between devices: 45.8 us -> 48.3 us
  other arithmetic: 2.2 us -> 3.96 us
    all_gather x1, waiting for transfers between devices: 7.52 us -> 3.47 us  [per_device(): hid = lax.all_gather(hidden, 'y')]
    dot_general x1 -> x0, matrix products: 3.29 us -> none  [per_device(): lax.dot_general(hid, cot, (((0, 1), (0, 1)), ((), ())), preferred_element...]
    pallas_call x3 -> x2, Pallas kernels: 18.6 us -> 15.5 us  [the longest x1 8.41 us: products(): pl.pallas_call(products_kernel, grid_spec=pltpu.PrefetchScalarGridSpec(nu...]
    ppermute x5 -> x7, starting transfers between devices: 25.9 us -> 28.7 us  [the longest x3 14.5 us: per_device(): lax.ppermute(others[d - 1], 'z_hi', ring(Z_HI, d))]
    convert_element_type x0 -> x1, other arithmetic: none -> 2.72 us  [per_device(): pair = (keep.astype(F32) + got.astype(F32)).astype(BF16)]
    ppermute x1, waiting for transfers between devices: 0.01 us -> 2.48 us  [per_device(): got = lax.ppermute(send, 'core', ring(CORE, 1))]
    reshape x2 -> x1, local copies, waits for them, and re-layouts: 2.54 us -> 0.8 us  [per_device(): mine.reshape(SHARE, Z_HI, Y, 128).transpose(2, 0, 1, 3)]
    ppermute x5 -> x7, waiting for transfers between devices: 17.8 us -> 16.3 us  [the longest x3 8.32 us: per_device(): lax.ppermute(others[d - 1], 'z_hi', ring(Z_HI, d))]
  transfers between devices with their start and end apart: 11 -> 13, of which waited for: 4 -> 7; matrix products, arithmetic and copies ran while one was open for 7% -> 5% of each run, Pallas kernels for 16% -> 15%
where the time goes in v3:
time: 134 us; the launch traced here: 133 us
  starting transfers between devices  48.3 us (36%)
  waiting for transfers between devices  23.5 us (18%)
  Pallas kernels  19.9 us (15%)
  blocking collectives  18.3 us (14%)
  between operations  14.3 us (11%)
  local copies, waits for them, and re-layouts  5.17 us (4%)
  other arithmetic  3.96 us (3%)
    all_gather x1, blocking collectives, per_device(): near = lax.all_gather(pack_block(packed_codes, block_scales), 'z_hi')  18.3 us
    ppermute x3, starting transfers between devices, per_device(): lax.ppermute(others[d - 1], 'z_hi', ring(Z_HI, d))  14.5 us
    ppermute x3, starting transfers between devices, per_device(): parts.append(lax.ppermute(mine, ('z_lo', 'x'), pairs))  8.84 us
    pallas_call x1, Pallas kernels, products(): pl.pallas_call(products_kernel, grid_spec=pltpu.PrefetchScalarGridSpec(nu...  8.41 us
    ppermute x3, waiting for transfers between devices, per_device(): lax.ppermute(others[d - 1], 'z_hi', ring(Z_HI, d))  8.32 us
    ppermute x3, waiting for transfers between devices, per_device(): parts.append(lax.ppermute(mine, ('z_lo', 'x'), pairs))  8 us
    all_to_all x1, starting transfers between devices, per_device(): mine = lax.all_to_all(mine, 'y', 0, 0)  7.65 us
    pallas_call x1, Pallas kernels, grad_hidden_of(): pl.pallas_call(grad_hidden_kernel, in_specs=[pl.BlockSpec(memory_space=pl...  7.08 us
  transfers between devices with their start and end apart: 13, of which 7 were waited for; matrix products, arithmetic and copies ran while one was open for 5% of the time, Pallas kernels for 15%

profile of v3, /device:TPU:1, one launch (start us, length us, event | category | flops | bytes accessed | tf_op | source)
XLA Modules:
  0.0 133.4 jit_solution(4330167439827476125)
XLA Ops:
  7.2 0.7 all-gather.6.cloned.1.call-update
  7.9 1.0 dynamic-slice_bitcast_fusion
  9.1 0.8 reshape.19
  9.9 7.7 %all-to-all-start = ((bf16[8,32,512]{2,1,0:T(8,128)(2,1)}), bf16[8,32,512]{2,1,0:T(8,128)(2,1)S(1)}, u32[]{:S(2)}, u32[]{:S(2)}) async-start(bf16[8,32,512]{2,1,0:T(8,128)(2,1)} %reshape.19), calls=%async_computation | async-start | bytes 524288 | tf_op jit(solution)/shard_map/all_to_all | solution.py:261
  17.8 18.3 %all-gather.1 = s32[480,128]{1,0:T(8,128)} all-gather(s32[120,128]{1,0:T(8,128)S(1)} %pad_add_fusion), channel_id=3, replica_groups=mesh['z_lo'=2,'x'=4,'core'=2,'z_hi'=4,'y'=8] {'z_hi'}, dimensions={0}, use_global_device_ids=true | all-gather | bytes 307200 | tf_op jit(solution)/shard_map/all_gather | solution.py:256
  36.1 3.1 %collective-permute-start.1 = (bf16[8,32,512]{2,1,0:T(8,128)(2,1)S(1)}, bf16[8,32,512]{2,1,0:T(8,128)(2,1)S(1)}, u32[]{:S(2)}, u32[]{:S(2)}) collective-permute-start(bf16[8,32,512]{2,1,0:T(8,128)(2,1)S(1)} %all-to-all-done.refs_0_), channel_id=1, source_target_pairs={{0,64},{64,0},{128,192},{192,128},{256,320},{320,256},{384,448},{4... | collective-permute-start | bytes 786440 | tf_op jit(solution)/shard_map/ppermute | solution.py:266
  39.2 3.8 %collective-permute-start.2 = (bf16[8,32,512]{2,1,0:T(8,128)(2,1)S(1)}, bf16[8,32,512]{2,1,0:T(8,128)(2,1)S(1)}, u32[]{:S(2)}, u32[]{:S(2)}) collective-permute-start(bf16[8,32,512]{2,1,0:T(8,128)(2,1)S(1)} %all-to-all-done.refs_0_), channel_id=1, source_target_pairs={{0,320},{64,256},{128,448},{192,384},{256,64},{320,0},{384,192},{4... | collective-permute-start | bytes 786440 | tf_op jit(solution)/shard_map/ppermute | solution.py:266
  43.0 1.9 %collective-permute-start = (bf16[8,32,512]{2,1,0:T(8,128)(2,1)S(1)}, bf16[8,32,512]{2,1,0:T(8,128)(2,1)S(1)}, u32[]{:S(2)}, u32[]{:S(2)}) collective-permute-start(bf16[8,32,512]{2,1,0:T(8,128)(2,1)S(1)} %all-to-all-done.refs_0_), channel_id=1, source_target_pairs={{0,256},{64,320},{128,384},{192,448},{256,0},{320,64},{384,128},{4... | collective-permute-start | bytes 786440 | tf_op jit(solution)/shard_map/ppermute | solution.py:266
  44.9 2.7 %collective-permute-done.2.refs_3_ = bf16[8,32,512]{2,1,0:T(8,128)(2,1)S(1)} collective-permute-done((bf16[8,32,512]{2,1,0:T(8,128)(2,1)S(1)}, bf16[8,32,512]{2,1,0:T(8,128)(2,1)S(1)}, u32[]{:S(2)}, u32[]{:S(2)}) %collective-permute-start.2) | collective-permute-done | bytes 262176 | tf_op jit(solution)/shard_map/ppermute | solution.py:266
  47.6 5.3 %collective-permute-done.refs_1_ = bf16[8,32,512]{2,1,0:T(8,128)(2,1)S(1)} collective-permute-done((bf16[8,32,512]{2,1,0:T(8,128)(2,1)S(1)}, bf16[8,32,512]{2,1,0:T(8,128)(2,1)S(1)}, u32[]{:S(2)}, u32[]{:S(2)}) %collective-permute-start) | collective-permute-done | bytes 262176 | tf_op jit(solution)/shard_map/ppermute | solution.py:266
  52.9 0.1 pad_maximum_fusion
  53.1 5.4 %collective-permute-start.3 = (bf16[4,8,32,512]{3,2,1,0:T(8,128)(2,1)S(1)}, bf16[4,8,32,512]{3,2,1,0:T(8,128)(2,1)S(1)}, u32[]{:S(2)}, u32[]{:S(2)}) collective-permute-start(bf16[4,8,32,512]{3,2,1,0:T(8,128)(2,1)S(1)} %pad_maximum_fusion), channel_id=1, source_target_pairs={{0,32},{32,0},{1,33},{33,1},{2,34},{34,2},{3,35},{35,3},{4,36},{36... | collective-permute-start | bytes 3145736 | tf_op jit(solution)/shard_map/ppermute | solution.py:268
  58.6 3.3 %shard_map.67.weight_ref = bf16[896,512]{1,0:T(8,128)(2,1)} custom-call(s32[4,120,128]{2,1,0:T(8,128)} %bitcast.32), custom_call_target="tpu_custom_call" | custom-call | flops 2000000 | bytes 1200000 | tf_op jit(solution)/shard_map/pallas_call | solution.py:52
  61.9 1.1 shard_map.68.cot_ref
  63.0 1.3 %copy-done = bf16[8,256,512]{2,1,0:T(8,128)(2,1)} copy-done((bf16[8,256,512]{2,1,0:T(8,128)(2,1)}, bf16[8,256,512]{2,1,0:T(8,128)(2,1)S(1)}, u32[]{:S(2)}) %copy-start) | copy-done | bytes 2097176
  64.4 3.5 %all-gather.6.cloned.1.call-done = bf16[2048,896]{1,0:T(8,128)(2,1)} async-done(((bf16[256,896]{1,0:T(8,128)(2,1)}), bf16[2048,896]{1,0:T(8,128)(2,1)}) %all-gather.6.cloned.1.call-update) | async-done | bytes 3670032 | tf_op jit(solution)/shard_map/all_gather | solution.py:255
  67.8 8.4 %shard_map.69 = (bf16[8,8,16,512]{3,2,1,0:T(8,128)(2,1)}, bf16[8,8,16,512]{3,2,1,0:T(8,128)(2,1)}, f32[128,896]{1,0:T(8,128)}, bf16[128,896]{1,0:T(8,128)(2,1)},...) custom-call(s32[4]{0:T(128)} %copy-done.1, bf16[8,256,896]{2,1,0:T(8,128)(2,1)} %bitcast.37, ...), custom_call_target="tpu_custom_call" | custom-call | flops 3758096384 | bytes 10000000 | tf_op jit(solution)/shard_map/pallas_call | solution.py:148
  76.3 2.6 %collective-permute-start.4 = (bf16[8,8,16,512]{3,2,1,0:T(8,128)(2,1)}, bf16[8,8,16,512]{3,2,1,0:T(8,128)(2,1)S(1)}, u32[]{:S(2)}, u32[]{:S(2)}) collective-permute-start(bf16[8,8,16,512]{3,2,1,0:T(8,128)(2,1)} %get-tuple-element.29), channel_id=1, source_target_pairs={{0,32},{32,0},{1,33},{33,1},{2,34},{34,2},{3,35},{35,3},{4,36},{36... | collective-permute-start | bytes 3145736 | tf_op jit(solution)/shard_map/ppermute | solution.py:273
  78.8 2.5 %collective-permute-done.4 = bf16[8,8,16,512]{3,2,1,0:T(8,128)(2,1)S(1)} collective-permute-done((bf16[8,8,16,512]{3,2,1,0:T(8,128)(2,1)}, bf16[8,8,16,512]{3,2,1,0:T(8,128)(2,1)S(1)}, u32[]{:S(2)}, u32[]{:S(2)}) %collective-permute-start.4) | collective-permute-done | bytes 1048608 | tf_op jit(solution)/shard_map/ppermute | solution.py:273
  81.3 2.7 %add_convert_fusion = bf16[8,8,16,512]{3,2,1,0:T(8,128)(2,1)} fusion(bf16[8,8,16,512]{3,2,1,0:T(8,128)(2,1)S(1)} %collective-permute-done.4, bf16[8,8,16,512]{3,2,1,0:T(8,128)(2,1)} %get-tuple-element.28), kind=kLoop, calls=%fused_computation | loop fusion | flops 2097152 | bytes 3145728 | tf_op jit(solution)/shard_map/convert_element_type | solution.py:274
  84.0 5.1 %all-to-all-start.1 = ((bf16[8,8,16,512]{3,2,1,0:T(8,128)(2,1)}), bf16[8,8,16,512]{3,2,1,0:T(8,128)(2,1)S(1)}, u32[]{:S(2)}, u32[]{:S(2)}) async-start(bf16[8,8,16,512]{3,2,1,0:T(8,128)(2,1)} %add_convert_fusion), calls=%async_computation.1 | async-start | bytes 2097152 | tf_op jit(solution)/shard_map/all_to_all | solution.py:279
  89.1 7.1 %collective-permute-start.5 = (bf16[128,896]{1,0:T(8,128)(2,1)S(1)}, bf16[128,896]{1,0:T(8,128)(2,1)S(1)}, u32[]{:S(2)}, u32[]{:S(2)}) collective-permute-start(bf16[128,896]{1,0:T(8,128)(2,1)S(1)} %copy-done.6), channel_id=1, source_target_pairs={{0,16},{8,24},{16,0},{24,8},{1,17},{9,25},{17,1},{25,9},{2,18},{10... | collective-permute-start | bytes 688136 | tf_op jit(solution)/shard_map/ppermute | solution.py:277
  96.2 2.7 %collective-permute-start.6 = (bf16[128,896]{1,0:T(8,128)(2,1)S(1)}, bf16[128,896]{1,0:T(8,128)(2,1)S(1)}, u32[]{:S(2)}, u32[]{:S(2)}) collective-permute-start(bf16[128,896]{1,0:T(8,128)(2,1)S(1)} %copy-done.5), channel_id=1, source_target_pairs={{0,8},{8,16},{16,24},{24,0},{1,9},{9,17},{17,25},{25,1},{2,10},{10... | collective-permute-start | bytes 688136 | tf_op jit(solution)/shard_map/ppermute | solution.py:277
  99.0 4.7 %collective-permute-start.7 = (bf16[128,896]{1,0:T(8,128)(2,1)S(1)}, bf16[128,896]{1,0:T(8,128)(2,1)S(1)}, u32[]{:S(2)}, u32[]{:S(2)}) collective-permute-start(bf16[128,896]{1,0:T(8,128)(2,1)S(1)} %copy-done.4), channel_id=1, source_target_pairs={{0,24},{8,0},{16,8},{24,16},{1,25},{9,1},{17,9},{25,17},{2,26},{10... | collective-permute-start | bytes 688136 | tf_op jit(solution)/shard_map/ppermute | solution.py:277
  103.6 0.5 all-to-all-done.1
  104.2 0.8 reduce_sum.12
  105.0 4.2 %all-to-all-start.2 = ((bf16[8,16,512]{2,1,0:T(8,128)(2,1)}), bf16[8,16,512]{2,1,0:T(8,128)(2,1)S(1)}, u32[]{:S(2)}, u32[]{:S(2)}) async-start(bf16[8,16,512]{2,1,0:T(8,128)(2,1)} %reduce_sum.12), calls=%async_computation.2 | async-start | bytes 262144 | tf_op jit(solution)/shard_map/all_to_all | solution.py:281
  109.2 7.1 %shard_map.70 = bf16[256,896]{1,0:T(8,128)(2,1)} custom-call(bf16[256,4096]{1,0:T(8,128)(2,1)} %cot_ref.1, s32[8,4,120,128]{3,2,1,0:T(8,128)} %bitcast.38), custom_call_target="tpu_custom_call" | custom-call | flops 1879048192 | bytes 6000000 | tf_op jit(solution)/shard_map/pallas_call | solution.py:226
  116.3 0.4 collective-permute-done.5
  116.7 7.9 %collective-permute-done.6 = bf16[128,896]{1,0:T(8,128)(2,1)S(1)} collective-permute-done((bf16[128,896]{1,0:T(8,128)(2,1)S(1)}, bf16[128,896]{1,0:T(8,128)(2,1)S(1)}, u32[]{:S(2)}, u32[]{:S(2)}) %collective-permute-start.6) | collective-permute-done | bytes 229408 | tf_op jit(solution)/shard_map/ppermute | solution.py:277
  124.7 1.0 copy.15
  125.8 0.7 copy.19
  (35 shorter events, 0.8 us)
Async XLA Ops:
  7.2 10.4 %copy-start.7 = (f32[7,1]{0,1:T(1,128)S(1)}, f32[7,1]{0,1:T(1,128)}, u32[]{:S(2)}) copy-start(f32[7,1]{0,1:T(1,128)} %param.7) | copy-start | bytes 88
  7.2 10.5 %copy-start.3 = (s32[224,128]{1,0:T(8,128)S(1)}, s32[224,128]{1,0:T(8,128)}, u32[]{:S(2)}) copy-start(s32[224,128]{1,0:T(8,128)} %param.6) | copy-start | bytes 344068
  7.2 60.7 %all-gather.6.cloned.1.call-start = ((), (), s32[]{:S(2)}) async-start(), calls=%async_computation.3 | async-start | bytes 4128768 | tf_op jit(solution)/shard_map/all_gather | solution.py:255
  9.9 26.2 %all-to-all-start = ((bf16[8,32,512]{2,1,0:T(8,128)(2,1)}), bf16[8,32,512]{2,1,0:T(8,128)(2,1)S(1)}, u32[]{:S(2)}, u32[]{:S(2)}) async-start(bf16[8,32,512]{2,1,0:T(8,128)(2,1)} %reshape.19), calls=%async_computation | async-start | bytes 524288 | tf_op jit(solution)/shard_map/all_to_all | solution.py:261
  17.5 91.7 %all-gather.8.cloned.1.call-start = ((), (), s32[]{:S(2)}) async-start(), calls=%async_computation.4 | async-start | bytes 2211840 | tf_op jit(solution)/shard_map/all_gather | solution.py:284
  36.1 8.9 %collective-permute-start.1 = (bf16[8,32,512]{2,1,0:T(8,128)(2,1)S(1)}, bf16[8,32,512]{2,1,0:T(8,128)(2,1)S(1)}, u32[]{:S(2)}, u32[]{:S(2)}) collective-permute-start(bf16[8,32,512]{2,1,0:T(8,128)(2,1)S(1)} %all-to-all-done.refs_0_), channel_id=1, source_target_pairs={{0,64},{64,0},{128,192},{192,128},{256,320},{320,256},{384,448},{4... | collective-permute-start | bytes 786440 | tf_op jit(solution)/shard_map/ppermute | solution.py:266
  39.2 8.5 %collective-permute-start.2 = (bf16[8,32,512]{2,1,0:T(8,128)(2,1)S(1)}, bf16[8,32,512]{2,1,0:T(8,128)(2,1)S(1)}, u32[]{:S(2)}, u32[]{:S(2)}) collective-permute-start(bf16[8,32,512]{2,1,0:T(8,128)(2,1)S(1)} %all-to-all-done.refs_0_), channel_id=1, source_target_pairs={{0,320},{64,256},{128,448},{192,384},{256,64},{320,0},{384,192},{4... | collective-permute-start | bytes 786440 | tf_op jit(solution)/shard_map/ppermute | solution.py:266
  43.0 10.0 %collective-permute-start = (bf16[8,32,512]{2,1,0:T(8,128)(2,1)S(1)}, bf16[8,32,512]{2,1,0:T(8,128)(2,1)S(1)}, u32[]{:S(2)}, u32[]{:S(2)}) collective-permute-start(bf16[8,32,512]{2,1,0:T(8,128)(2,1)S(1)} %all-to-all-done.refs_0_), channel_id=1, source_target_pairs={{0,256},{64,320},{128,384},{192,448},{256,0},{320,64},{384,128},{4... | collective-permute-start | bytes 786440 | tf_op jit(solution)/shard_map/ppermute | solution.py:266
  53.1 8.8 %collective-permute-start.3 = (bf16[4,8,32,512]{3,2,1,0:T(8,128)(2,1)S(1)}, bf16[4,8,32,512]{3,2,1,0:T(8,128)(2,1)S(1)}, u32[]{:S(2)}, u32[]{:S(2)}) collective-permute-start(bf16[4,8,32,512]{3,2,1,0:T(8,128)(2,1)S(1)} %pad_maximum_fusion), channel_id=1, source_target_pairs={{0,32},{32,0},{1,33},{33,1},{2,34},{34,2},{3,35},{35,3},{4,36},{36... | collective-permute-start | bytes 3145736 | tf_op jit(solution)/shard_map/ppermute | solution.py:268
  58.5 4.5 %copy-start.1 = (s32[4]{0:T(128)}, s32[4]{0:T(128)S(1)}, u32[]{:S(2)}) copy-start(s32[4]{0:T(128)S(1)} %pad_add_fusion.1.place_ref) | copy-start | bytes 52
  63.0 1.3 %copy-start = (bf16[8,256,512]{2,1,0:T(8,128)(2,1)}, bf16[8,256,512]{2,1,0:T(8,128)(2,1)S(1)}, u32[]{:S(2)}) copy-start(bf16[8,256,512]{2,1,0:T(8,128)(2,1)S(1)} %shard_map.68.cot_ref) | copy-start | bytes 6291460
  76.3 5.1 %collective-permute-start.4 = (bf16[8,8,16,512]{3,2,1,0:T(8,128)(2,1)}, bf16[8,8,16,512]{3,2,1,0:T(8,128)(2,1)S(1)}, u32[]{:S(2)}, u32[]{:S(2)}) collective-permute-start(bf16[8,8,16,512]{3,2,1,0:T(8,128)(2,1)} %get-tuple-element.29), channel_id=1, source_target_pairs={{0,32},{32,0},{1,33},{33,1},{2,34},{34,2},{3,35},{35,3},{4,36},{36... | collective-permute-start | bytes 3145736 | tf_op jit(solution)/shard_map/ppermute | solution.py:273
  81.3 7.8 %copy-start.6 = (bf16[128,896]{1,0:T(8,128)(2,1)S(1)}, bf16[128,896]{1,0:T(8,128)(2,1)}, u32[]{:S(2)}) copy-start(bf16[128,896]{1,0:T(8,128)(2,1)} %get-tuple-element.35) | copy-start | bytes 688132
  81.3 14.9 %copy-start.5 = (bf16[128,896]{1,0:T(8,128)(2,1)S(1)}, bf16[128,896]{1,0:T(8,128)(2,1)}, u32[]{:S(2)}) copy-start(bf16[128,896]{1,0:T(8,128)(2,1)} %get-tuple-element.36) | copy-start | bytes 688132
  81.3 17.6 %copy-start.4 = (bf16[128,896]{1,0:T(8,128)(2,1)S(1)}, bf16[128,896]{1,0:T(8,128)(2,1)}, u32[]{:S(2)}) copy-start(bf16[128,896]{1,0:T(8,128)(2,1)} %get-tuple-element.37) | copy-start | bytes 688132
  84.0 20.1 %all-to-all-start.1 = ((bf16[8,8,16,512]{3,2,1,0:T(8,128)(2,1)}), bf16[8,8,16,512]{3,2,1,0:T(8,128)(2,1)S(1)}, u32[]{:S(2)}, u32[]{:S(2)}) async-start(bf16[8,8,16,512]{3,2,1,0:T(8,128)(2,1)} %add_convert_fusion), calls=%async_computation.1 | async-start | bytes 2097152 | tf_op jit(solution)/shard_map/all_to_all | solution.py:279
  89.1 27.6 %collective-permute-start.5 = (bf16[128,896]{1,0:T(8,128)(2,1)S(1)}, bf16[128,896]{1,0:T(8,128)(2,1)S(1)}, u32[]{:S(2)}, u32[]{:S(2)}) collective-permute-start(bf16[128,896]{1,0:T(8,128)(2,1)S(1)} %copy-done.6), channel_id=1, source_target_pairs={{0,16},{8,24},{16,0},{24,8},{1,17},{9,25},{17,1},{25,9},{2,18},{10... | collective-permute-start | bytes 688136 | tf_op jit(solution)/shard_map/ppermute | solution.py:277
  96.2 28.4 %collective-permute-start.6 = (bf16[128,896]{1,0:T(8,128)(2,1)S(1)}, bf16[128,896]{1,0:T(8,128)(2,1)S(1)}, u32[]{:S(2)}, u32[]{:S(2)}) collective-permute-start(bf16[128,896]{1,0:T(8,128)(2,1)S(1)} %copy-done.5), channel_id=1, source_target_pairs={{0,8},{8,16},{16,24},{24,0},{1,9},{9,17},{17,25},{25,1},{2,10},{10... | collective-permute-start | bytes 688136 | tf_op jit(solution)/shard_map/ppermute | solution.py:277
  99.0 25.7 %collective-permute-start.7 = (bf16[128,896]{1,0:T(8,128)(2,1)S(1)}, bf16[128,896]{1,0:T(8,128)(2,1)S(1)}, u32[]{:S(2)}, u32[]{:S(2)}) collective-permute-start(bf16[128,896]{1,0:T(8,128)(2,1)S(1)} %copy-done.4), channel_id=1, source_target_pairs={{0,24},{8,0},{16,8},{24,16},{1,25},{9,1},{17,9},{25,17},{2,26},{10... | collective-permute-start | bytes 688136 | tf_op jit(solution)/shard_map/ppermute | solution.py:277
  105.0 20.7 %all-to-all-start.2 = ((bf16[8,16,512]{2,1,0:T(8,128)(2,1)}), bf16[8,16,512]{2,1,0:T(8,128)(2,1)S(1)}, u32[]{:S(2)}, u32[]{:S(2)}) async-start(bf16[8,16,512]{2,1,0:T(8,128)(2,1)} %reduce_sum.12), calls=%async_computation.2 | async-start | bytes 262144 | tf_op jit(solution)/shard_map/all_to_all | solution.py:281
  109.2 15.4 %copy-start.2 = (f32[128,896]{1,0:T(8,128)S(1)}, f32[128,896]{1,0:T(8,128)}, u32[]{:S(2)}) copy-start(f32[128,896]{1,0:T(8,128)} %get-tuple-element.39) | copy-start | bytes 1376260
Sparse Core Ops, SparseCore 0:
  10.1 57.6 all-gather.5
  69.9 38.6 all-gather.7

commit v4 on v3

--- a/solution.py
+++ b/solution.py
@@ -14,10 +14,12 @@
 HIDDEN_DEV = 896
 SCALE_ROWS = 8
 CHUNKS = 4
+HALVES = 4
 SHARE = 32
 EXACT = 2.0**34
 SIGNS = -0x77777778
 VMEM_BYTES = 56 * 1024 * 1024
+VMEM_PRODUCTS = 50 * 1024 * 1024
 
 
 def pack_block(codes, scales):
@@ -87,30 +89,25 @@
         ),
         out_shape=jax.ShapeDtypeStruct((groups, 8 * share, width), BF16),
         cost_estimate=pl.CostEstimate(flops=0, bytes_accessed=4_000_000, transcendentals=0),
-        compiler_params=pltpu.CompilerParams(vmem_limit_bytes=32 * 1024 * 1024),
+        compiler_params=pltpu.CompilerParams(vmem_limit_bytes=VMEM_BYTES),
     )(place, *parts, other)
 
 
-def products_kernel(
-    place_ref, hid_ref, weight_ref, cot_ref, keep_ref, send_ref, own_ref, up_ref, far_ref, down_ref,
-    hid, weight, cot, keep, send, sems, out_sems,
-):
+def outputs_kernel(place_ref, hid_ref, weight_ref, keep_ref, send_ref, hid, weight, keep, send, sems, out_sems):
     core = place_ref[0]
-    chunks = CHUNKS
     groups, rows, depth = hid.shape
-    step, width = groups // chunks, weight.shape[1]
-    load_weight = pltpu.make_async_copy(weight_ref, weight, sems.at[chunks])
-    load_cot = pltpu.make_async_copy(cot_ref, cot, sems.at[chunks + 1])
+    step, width = groups // CHUNKS, weight.shape[1]
+    load_weight = pltpu.make_async_copy(weight_ref, weight, sems.at[CHUNKS])
     loads = [
         pltpu.make_async_copy(hid_ref.at[pl.ds(i * step, step)], hid.at[pl.ds(i * step, step)], sems.at[i])
-        for i in range(chunks)
+        for i in range(CHUNKS)
     ]
     load_weight.start()
     for load in loads:
         load.start()
-    load_cot.start()
     load_weight.wait()
-    for i in range(chunks):
+    stores = []
+    for i in range(CHUNKS):
         loads[i].wait()
         product = jnp.dot(
             hid[i * step : (i + 1) * step].reshape(step * rows, depth), weight[...], preferred_element_type=F32
@@ -120,56 +117,88 @@
             first, second = product[g, :, 0], product[g, :, 1]
             keep[:, i * step + g] = jnp.where(core == 0, first, second)
             send[:, i * step + g] = jnp.where(core == 0, second, first)
-    stores = [
-        pltpu.make_async_copy(send, send_ref, out_sems.at[0]),
-        pltpu.make_async_copy(keep, keep_ref, out_sems.at[1]),
-    ]
-    for store in stores:
-        store.start()
-    load_cot.wait()
-    tokens = hid[...].reshape(groups * rows, depth)
-    columns = cot[...].reshape(groups * rows, width)
-
-    def term(i):
-        part = columns[:, i * 128 : (i + 1) * 128]
-        return lax.dot_general(part, tokens, (((0,), (0,)), ((), ())), preferred_element_type=F32)
-
-    for i, ref in enumerate((own_ref, up_ref, far_ref, down_ref)):
-        ref[...] = term(i).astype(ref.dtype)
+        at = pl.ds(i * step, step)
+        stores.append(pltpu.make_async_copy(send.at[:, at], send_ref.at[:, at], out_sems.at[0, i]))
+        stores.append(pltpu.make_async_copy(keep.at[:, at], keep_ref.at[:, at], out_sems.at[1, i]))
+        for store in stores[-2:]:
+            store.start()
     for store in stores:
         store.wait()
 
 
-def products(place, hid, weight, cot):
+def ring_outputs(place, hid, weight):
     groups, _, depth = hid.shape
     width = weight.shape[1]
     part = (Z_LO * X, groups, 16, width)
-    anywhere, vmem = pl.BlockSpec(memory_space=pl.ANY), pl.BlockSpec(memory_space=pltpu.VMEM)
-    return pl.pallas_call(
-        products_kernel,
+    anywhere = pl.BlockSpec(memory_space=pl.ANY)
+    return pl.pallas_call(
+        outputs_kernel,
         grid_spec=pltpu.PrefetchScalarGridSpec(
             num_scalar_prefetch=1,
             grid=(1,),
-            in_specs=[anywhere] * 3,
-            out_specs=[anywhere] * 2 + [vmem] * 4,
+            in_specs=[anywhere] * 2,
+            out_specs=[anywhere] * 2,
             scratch_shapes=[
                 pltpu.VMEM(hid.shape, BF16),
                 pltpu.VMEM(weight.shape, BF16),
-                pltpu.VMEM(cot.shape, BF16),
                 pltpu.VMEM(part, BF16),
                 pltpu.VMEM(part, BF16),
-                pltpu.SemaphoreType.DMA((CHUNKS + 2,)),
-                pltpu.SemaphoreType.DMA((2,)),
+                pltpu.SemaphoreType.DMA((CHUNKS + 1,)),
+                pltpu.SemaphoreType.DMA((2, CHUNKS)),
             ],
         ),
-        out_shape=[jax.ShapeDtypeStruct(part, BF16)] * 2
-        + [jax.ShapeDtypeStruct((128, depth), F32)]
-        + [jax.ShapeDtypeStruct((128, depth), BF16)] * 3,
+        out_shape=[jax.ShapeDtypeStruct(part, BF16)] * 2,
         cost_estimate=pl.CostEstimate(
-            flops=4 * groups * 256 * depth * width, bytes_accessed=10_000_000, transcendentals=0
-        ),
-        compiler_params=pltpu.CompilerParams(vmem_limit_bytes=VMEM_BYTES),
-    )(place, hid, weight, cot)
+            flops=2 * groups * 256 * depth * width, bytes_accessed=7_000_000, transcendentals=0
+        ),
+        compiler_params=pltpu.CompilerParams(vmem_limit_bytes=VMEM_PRODUCTS),
+    )(place, hid, weight)
+
+
+def terms_kernel(hid_ref, cot_ref, own_ref, up_ref, far_ref, down_ref, hid, cot, sems):
+    groups, rows, depth = hid.shape
+    step, width = groups // HALVES, cot.shape[2]
+    loads = []
+    for i in range(HALVES):
+        at = pl.ds(i * step, step)
+        loads.append(pltpu.make_async_copy(cot_ref.at[at], cot.at[at], sems.at[0, i]))
+        loads.append(pltpu.make_async_copy(hid_ref.at[at], hid.at[at], sems.at[1, i]))
+    for load in loads:
+        load.start()
+    total = None
+    for i in range(HALVES):
+        loads[2 * i].wait()
+        loads[2 * i + 1].wait()
+        part = slice(i * step, (i + 1) * step)
+        term = lax.dot_general(
+            cot[part].reshape(step * rows, width),
+            hid[part].reshape(step * rows, depth),
+            (((0,), (0,)), ((), ())),
+            preferred_element_type=F32,
+        )
+        total = term if total is None else total + term
+    for i, ref in enumerate((own_ref, up_ref, far_ref, down_ref)):
+        ref[...] = total[i * 128 : (i + 1) * 128].astype(BF16)
+
+
+def gradient_terms(hid, cot):
+    groups, rows, depth = hid.shape
+    width = cot.shape[2]
+    return pl.pallas_call(
+        terms_kernel,
+        in_specs=[pl.BlockSpec(memory_space=pl.ANY)] * 2,
+        out_specs=[pl.BlockSpec(memory_space=pltpu.VMEM)] * 4,
+        scratch_shapes=[
+            pltpu.VMEM(hid.shape, BF16),
+            pltpu.VMEM(cot.shape, BF16),
+            pltpu.SemaphoreType.DMA((2, HALVES)),
+        ],
+        out_shape=[jax.ShapeDtypeStruct((128, depth), BF16)] * 4,
+        cost_estimate=pl.CostEstimate(
+            flops=2 * groups * rows * depth * width, bytes_accessed=7_000_000, transcendentals=0
+        ),
+        compiler_params=pltpu.CompilerParams(vmem_limit_bytes=VMEM_PRODUCTS),
+    )(hid, cot)
 
 
 def row_widths(part):
@@ -268,9 +297,12 @@
     other = lax.ppermute(jnp.stack(parts), "core", ring(CORE, 1))
     cot = assemble(place, parts, other)
     hid, weight, cot = lax.optimization_barrier((hid, weight, cot))
-    keep, send, own, *others = products(place, hid, weight, cot)
+    keep, send = ring_outputs(place, hid, weight)
 
     got = lax.ppermute(send, "core", ring(CORE, 1))
+    hid, cot, send = lax.optimization_barrier((hid, cot, send))
+    own, *others = gradient_terms(hid, cot)
+    got, own, *others = lax.optimization_barrier((got, own, *others))
     pair = (keep.astype(F32) + got.astype(F32)).astype(BF16)
 
     pair, *others = lax.optimization_barrier((pair, *others))
@@ -285,7 +317,7 @@
     every, rows = lax.optimization_barrier((every, rows))
     grad_hidden = grad_hidden_of(cotangent, every)
     grad_hidden, *terms = lax.optimization_barrier((grad_hidden, *terms))
-    grad_weight = (own + sum(term.astype(F32) for term in terms)).T
+    grad_weight = sum(term.astype(F32) for term in (own, *terms)).T
     return output, grad_hidden, grad_weight
 
 

time: 134 us -> 133 us (level); the launches traced: 133 us -> 131 us
  waiting for transfers between devices: 23.5 us -> 17.3 us
  Pallas kernels: 19.9 us -> 23 us
    all_gather x1, waiting for transfers between devices: 3.47 us -> 0.26 us  [per_device(): hid = lax.all_gather(hidden, 'y')]
    ppermute x1, waiting for transfers between devices: 2.48 us -> 0.01 us  [per_device(): got = lax.ppermute(send, 'core', ring(CORE, 1))]
    pallas_call x1, Pallas kernels: 1.15 us -> 3.52 us  [assemble(): pl.pallas_call(assemble_kernel, grid_spec=pltpu.PrefetchScalarGridSpec(nu...]
    ppermute x3, waiting for transfers between devices: 8.32 us -> 6.45 us  [per_device(): lax.ppermute(others[d - 1], 'z_hi', ring(Z_HI, d))]
    all_gather x1, waiting for transfers between devices: 0.01 us -> 1.41 us  [per_device(): every = lax.all_gather(near, 'y')]
    pallas_call x1 -> x2, Pallas kernels: 8.41 us -> 9.15 us  [the longest x1 5.06 us: ring_outputs(): pl.pallas_call(outputs_kernel, grid_spec=pltpu.PrefetchScalarGridSpec(num...]
    unnamed x20 -> x24, local copies, waits for them, and re-layouts: 4.06 us -> 4.45 us
  transfers between devices with their start and end apart: 13 -> 13, of which waited for: 7 -> 6; matrix products, arithmetic and copies ran while one was open for 5% -> 5% of each run, Pallas kernels for 15% -> 18%
where the time goes in v4:
time: 133 us; the launch traced here: 131 us
  starting transfers between devices  49.3 us (37%)
  Pallas kernels  23 us (17%)
  blocking collectives  18.3 us (14%)
  waiting for transfers between devices  17.3 us (13%)
  between operations  14.3 us (11%)
  local copies, waits for them, and re-layouts  5.56 us (4%)
  other arithmetic  3.17 us (2%)
    all_gather x1, blocking collectives, per_device(): near = lax.all_gather(pack_block(packed_codes, block_scales), 'z_hi')  18.3 us
    ppermute x3, starting transfers between devices, per_device(): lax.ppermute(others[d - 1], 'z_hi', ring(Z_HI, d))  14.5 us
    ppermute x3, starting transfers between devices, per_device(): parts.append(lax.ppermute(mine, ('z_lo', 'x'), pairs))  8.85 us
    ppermute x3, waiting for transfers between devices, per_device(): parts.append(lax.ppermute(mine, ('z_lo', 'x'), pairs))  7.99 us
    all_to_all x1, starting transfers between devices, per_device(): mine = lax.all_to_all(mine, 'y', 0, 0)  7.65 us
    pallas_call x1, Pallas kernels, grad_hidden_of(): pl.pallas_call(grad_hidden_kernel, in_specs=[pl.BlockSpec(memory_space=pl...  7.04 us
    ppermute x3, waiting for transfers between devices, per_device(): lax.ppermute(others[d - 1], 'z_hi', ring(Z_HI, d))  6.45 us
    ppermute x1, starting transfers between devices, per_device(): other = lax.ppermute(jnp.stack(parts), 'core', ring(CORE, 1))  5.37 us
  transfers between devices with their start and end apart: 13, of which 6 were waited for; matrix products, arithmetic and copies ran while one was open for 5% of the time, Pallas kernels for 18%

profile of v4, /device:TPU:1, one launch (start us, length us, event | category | flops | bytes accessed | tf_op | source)
XLA Modules:
  0.0 130.8 jit_solution(536168261995104553)
XLA Ops:
  7.2 0.7 all-gather.6.cloned.1.call-update
  7.9 1.0 dynamic-slice_bitcast_fusion
  9.1 0.8 reshape.19
  9.9 7.7 %all-to-all-start = ((bf16[8,32,512]{2,1,0:T(8,128)(2,1)}), bf16[8,32,512]{2,1,0:T(8,128)(2,1)S(1)}, u32[]{:S(2)}, u32[]{:S(2)}) async-start(bf16[8,32,512]{2,1,0:T(8,128)(2,1)} %reshape.19), calls=%async_computation | async-start | bytes 524288 | tf_op jit(solution)/shard_map/all_to_all | solution.py:290
  17.8 18.3 %all-gather.1 = s32[480,128]{1,0:T(8,128)} all-gather(s32[120,128]{1,0:T(8,128)S(1)} %pad_add_fusion), channel_id=3, replica_groups=mesh['z_lo'=2,'x'=4,'core'=2,'z_hi'=4,'y'=8] {'z_hi'}, dimensions={0}, use_global_device_ids=true | all-gather | bytes 307200 | tf_op jit(solution)/shard_map/all_gather | solution.py:285
  36.1 3.1 %collective-permute-start.1 = (bf16[8,32,512]{2,1,0:T(8,128)(2,1)S(1)}, bf16[8,32,512]{2,1,0:T(8,128)(2,1)S(1)}, u32[]{:S(2)}, u32[]{:S(2)}) collective-permute-start(bf16[8,32,512]{2,1,0:T(8,128)(2,1)S(1)} %all-to-all-done.refs_0_), channel_id=1, source_target_pairs={{0,64},{64,0},{128,192},{192,128},{256,320},{320,256},{384,448},{4... | collective-permute-start | bytes 786440 | tf_op jit(solution)/shard_map/ppermute | solution.py:295
  39.2 3.8 %collective-permute-start.2 = (bf16[8,32,512]{2,1,0:T(8,128)(2,1)S(1)}, bf16[8,32,512]{2,1,0:T(8,128)(2,1)S(1)}, u32[]{:S(2)}, u32[]{:S(2)}) collective-permute-start(bf16[8,32,512]{2,1,0:T(8,128)(2,1)S(1)} %all-to-all-done.refs_0_), channel_id=1, source_target_pairs={{0,320},{64,256},{128,448},{192,384},{256,64},{320,0},{384,192},{4... | collective-permute-start | bytes 786440 | tf_op jit(solution)/shard_map/ppermute | solution.py:295
  43.0 1.9 %collective-permute-start = (bf16[8,32,512]{2,1,0:T(8,128)(2,1)S(1)}, bf16[8,32,512]{2,1,0:T(8,128)(2,1)S(1)}, u32[]{:S(2)}, u32[]{:S(2)}) collective-permute-start(bf16[8,32,512]{2,1,0:T(8,128)(2,1)S(1)} %all-to-all-done.refs_0_), channel_id=1, source_target_pairs={{0,256},{64,320},{128,384},{192,448},{256,0},{320,64},{384,128},{4... | collective-permute-start | bytes 786440 | tf_op jit(solution)/shard_map/ppermute | solution.py:295
  45.0 2.7 %collective-permute-done.2.refs_3_ = bf16[8,32,512]{2,1,0:T(8,128)(2,1)S(1)} collective-permute-done((bf16[8,32,512]{2,1,0:T(8,128)(2,1)S(1)}, bf16[8,32,512]{2,1,0:T(8,128)(2,1)S(1)}, u32[]{:S(2)}, u32[]{:S(2)}) %collective-permute-start.2) | collective-permute-done | bytes 262176 | tf_op jit(solution)/shard_map/ppermute | solution.py:295
  47.7 5.3 %collective-permute-done.refs_1_ = bf16[8,32,512]{2,1,0:T(8,128)(2,1)S(1)} collective-permute-done((bf16[8,32,512]{2,1,0:T(8,128)(2,1)S(1)}, bf16[8,32,512]{2,1,0:T(8,128)(2,1)S(1)}, u32[]{:S(2)}, u32[]{:S(2)}) %collective-permute-start) | collective-permute-done | bytes 262176 | tf_op jit(solution)/shard_map/ppermute | solution.py:295
  53.0 0.7 copy-done.7
  53.8 5.4 %collective-permute-start.3 = (bf16[4,8,32,512]{3,2,1,0:T(8,128)(2,1)S(1)}, bf16[4,8,32,512]{3,2,1,0:T(8,128)(2,1)S(1)}, u32[]{:S(2)}, u32[]{:S(2)}) collective-permute-start(bf16[4,8,32,512]{3,2,1,0:T(8,128)(2,1)S(1)} %pad_maximum_fusion), channel_id=1, source_target_pairs={{0,32},{32,0},{1,33},{33,1},{2,34},{34,2},{3,35},{35,3},{4,36},{36... | collective-permute-start | bytes 3145736 | tf_op jit(solution)/shard_map/ppermute | solution.py:297
  59.2 0.6 pad_add_fusion.1.place_ref
  59.7 3.2 %shard_map.67.weight_ref = bf16[896,512]{1,0:T(8,128)(2,1)} custom-call(s32[4,120,128]{2,1,0:T(8,128)} %bitcast.29), custom_call_target="tpu_custom_call" | custom-call | flops 2000000 | bytes 1200000 | tf_op jit(solution)/shard_map/pallas_call | solution.py:54
  63.0 1.0 copy-done.4
  64.1 3.5 %shard_map.68.cot_ref = bf16[8,256,512]{2,1,0:T(8,128)(2,1)} custom-call(s32[4]{0:T(128)} %pad_add_fusion.1.place_ref, bf16[8,32,512]{2,1,0:T(8,128)(2,1)} %copy-done.3, bf16[8,32,512]{2,1,0:T(8,128)(2,1)} %copy-done.7, bf16[8,32,512]{2,1,0:T(8,128)(2,1)} %copy-done.5, bf16[8,32,512]{2,1,0:T(8,128)(2,1)} %copy-done.6, bf16[4,8,32,512]{3,2,1,0:T(8,128)(2,1)} %copy-done.4), custom_call_target="tpu_custom_call" | custom-call | bytes 4000000 | tf_op jit(solution)/shard_map/pallas_call | solution.py:82
  67.8 5.1 %shard_map.69 = (bf16[8,8,16,512]{3,2,1,0:T(8,128)(2,1)S(1)}, bf16[8,8,16,512]{3,2,1,0:T(8,128)(2,1)S(1)}) custom-call(s32[4]{0:T(128)S(1)} %copy-done.2, bf16[8,256,896]{2,1,0:T(8,128)(2,1)} %bitcast.37, bf16[896,512]{1,0:T(8,128)(2,1)S(1)} %copy-done.1), custom_call_target="tpu_custom_call" | custom-call | flops 1879048192 | bytes 7000000 | tf_op jit(solution)/shard_map/pallas_call | solution.py:134
  72.9 2.6 %collective-permute-start.4 = (bf16[8,8,16,512]{3,2,1,0:T(8,128)(2,1)S(1)}, bf16[8,8,16,512]{3,2,1,0:T(8,128)(2,1)S(1)}, u32[]{:S(2)}, u32[]{:S(2)}) collective-permute-start(bf16[8,8,16,512]{3,2,1,0:T(8,128)(2,1)S(1)} %get-tuple-element.35), channel_id=1, source_target_pairs={{0,32},{32,0},{1,33},{33,1},{2,34},{34,2},{3,35},{35,3},{4,36},{36... | collective-permute-start | bytes 3145736 | tf_op jit(solution)/shard_map/ppermute | solution.py:302
  75.5 4.1 %shard_map.70 = (bf16[128,896]{1,0:T(8,128)(2,1)S(1)}, bf16[128,896]{1,0:T(8,128)(2,1)S(1)}, bf16[128,896]{1,0:T(8,128)(2,1)S(1)}, bf16[128,896]{1,0:T(8,128)(2,1)S(1)}) custom-call(bf16[8,256,896]{2,1,0:T(8,128)(2,1)} %bitcast.38, bf16[8,256,512]{2,1,0:T(8,128)(2,1)S(1)} %copy-done), custom_call_target="tpu_custom_call" | custom-call | flops 1879048192 | bytes 7000000 | tf_op jit(solution)/shard_map/pallas_call | solution.py:187
  79.6 1.4 %add_convert_fusion = bf16[8,8,16,512]{3,2,1,0:T(8,128)(2,1)} fusion(bf16[8,8,16,512]{3,2,1,0:T(8,128)(2,1)S(1)} %collective-permute-done.4, bf16[8,8,16,512]{3,2,1,0:T(8,128)(2,1)S(1)} %get-tuple-element.34), kind=kLoop, calls=%fused_computation | loop fusion | flops 2097152 | bytes 3145728 | tf_op jit(solution)/shard_map/convert_element_type | solution.py:306
  81.1 5.1 %all-to-all-start.1 = ((bf16[8,8,16,512]{3,2,1,0:T(8,128)(2,1)}), bf16[8,8,16,512]{3,2,1,0:T(8,128)(2,1)S(1)}, u32[]{:S(2)}, u32[]{:S(2)}) async-start(bf16[8,8,16,512]{3,2,1,0:T(8,128)(2,1)} %add_convert_fusion), calls=%async_computation.1 | async-start | bytes 2097152 | tf_op jit(solution)/shard_map/all_to_all | solution.py:311
  86.1 7.1 %collective-permute-start.5 = (bf16[128,896]{1,0:T(8,128)(2,1)S(1)}, bf16[128,896]{1,0:T(8,128)(2,1)S(1)}, u32[]{:S(2)}, u32[]{:S(2)}) collective-permute-start(bf16[128,896]{1,0:T(8,128)(2,1)S(1)} %get-tuple-element.49), channel_id=1, source_target_pairs={{0,16},{8,24},{16,0},{24,8},{1,17},{9,25},{17,1},{25,9},{2,18},{10... | collective-permute-start | bytes 688136 | tf_op jit(solution)/shard_map/ppermute | solution.py:309
  93.2 2.7 %collective-permute-start.6 = (bf16[128,896]{1,0:T(8,128)(2,1)S(1)}, bf16[128,896]{1,0:T(8,128)(2,1)S(1)}, u32[]{:S(2)}, u32[]{:S(2)}) collective-permute-start(bf16[128,896]{1,0:T(8,128)(2,1)S(1)} %get-tuple-element.50), channel_id=1, source_target_pairs={{0,8},{8,16},{16,24},{24,0},{1,9},{9,17},{17,25},{25,1},{2,10},{10... | collective-permute-start | bytes 688136 | tf_op jit(solution)/shard_map/ppermute | solution.py:309
  95.9 4.7 %collective-permute-start.7 = (bf16[128,896]{1,0:T(8,128)(2,1)S(1)}, bf16[128,896]{1,0:T(8,128)(2,1)S(1)}, u32[]{:S(2)}, u32[]{:S(2)}) collective-permute-start(bf16[128,896]{1,0:T(8,128)(2,1)S(1)} %get-tuple-element.51), channel_id=1, source_target_pairs={{0,24},{8,0},{16,8},{24,16},{1,25},{9,1},{17,9},{25,17},{2,26},{10... | collective-permute-start | bytes 688136 | tf_op jit(solution)/shard_map/ppermute | solution.py:309
  100.6 0.5 all-to-all-done.1
  101.1 0.8 reduce_sum.12
  102.0 5.2 %all-to-all-start.2 = ((bf16[8,16,512]{2,1,0:T(8,128)(2,1)}), bf16[8,16,512]{2,1,0:T(8,128)(2,1)S(1)}, u32[]{:S(2)}, u32[]{:S(2)}) async-start(bf16[8,16,512]{2,1,0:T(8,128)(2,1)} %reduce_sum.12), calls=%async_computation.2 | async-start | bytes 262144 | tf_op jit(solution)/shard_map/all_to_all | solution.py:313
  107.2 1.4 %all-gather.8.cloned.1.call-done = s32[32,120,128]{2,1,0:T(8,128)} async-done(((s32[4,120,128]{2,1,0:T(8,128)}), s32[32,120,128]{2,1,0:T(8,128)}) %all-gather.8.cloned.1.call-update) | async-done | bytes 1966096 | tf_op jit(solution)/shard_map/all_gather | solution.py:316
  108.6 7.0 %shard_map.71 = bf16[256,896]{1,0:T(8,128)(2,1)} custom-call(bf16[256,4096]{1,0:T(8,128)(2,1)} %cot_ref.1, s32[8,4,120,128]{3,2,1,0:T(8,128)} %bitcast.39), custom_call_target="tpu_custom_call" | custom-call | flops 1879048192 | bytes 6000000 | tf_op jit(solution)/shard_map/pallas_call | solution.py:255
  115.6 6.4 %collective-permute-done.6 = bf16[128,896]{1,0:T(8,128)(2,1)S(1)} collective-permute-done((bf16[128,896]{1,0:T(8,128)(2,1)S(1)}, bf16[128,896]{1,0:T(8,128)(2,1)S(1)}, u32[]{:S(2)}, u32[]{:S(2)}) %collective-permute-start.6) | collective-permute-done | bytes 229408 | tf_op jit(solution)/shard_map/ppermute | solution.py:309
  122.2 1.0 copy.15
  123.3 0.7 copy.19
  (40 shorter events, 1.1 us)
Async XLA Ops:
  7.2 10.4 %copy-start.9 = (f32[7,1]{0,1:T(1,128)S(1)}, f32[7,1]{0,1:T(1,128)}, u32[]{:S(2)}) copy-start(f32[7,1]{0,1:T(1,128)} %param.7) | copy-start | bytes 88
  7.2 10.5 %copy-start.8 = (s32[224,128]{1,0:T(8,128)S(1)}, s32[224,128]{1,0:T(8,128)}, u32[]{:S(2)}) copy-start(s32[224,128]{1,0:T(8,128)} %param.6) | copy-start | bytes 344068
  7.2 60.7 %all-gather.6.cloned.1.call-start = ((), (), s32[]{:S(2)}) async-start(), calls=%async_computation.3 | async-start | bytes 4128768 | tf_op jit(solution)/shard_map/all_gather | solution.py:284
  9.9 26.2 %all-to-all-start = ((bf16[8,32,512]{2,1,0:T(8,128)(2,1)}), bf16[8,32,512]{2,1,0:T(8,128)(2,1)S(1)}, u32[]{:S(2)}, u32[]{:S(2)}) async-start(bf16[8,32,512]{2,1,0:T(8,128)(2,1)} %reshape.19), calls=%async_computation | async-start | bytes 524288 | tf_op jit(solution)/shard_map/all_to_all | solution.py:290
  17.5 91.0 %all-gather.8.cloned.1.call-start = ((), (), s32[]{:S(2)}) async-start(), calls=%async_computation.4 | async-start | bytes 2211840 | tf_op jit(solution)/shard_map/all_gather | solution.py:316
  36.1 26.9 %copy-start.3 = (bf16[8,32,512]{2,1,0:T(8,128)(2,1)}, bf16[8,32,512]{2,1,0:T(8,128)(2,1)S(1)}, u32[]{:S(2)}) copy-start(bf16[8,32,512]{2,1,0:T(8,128)(2,1)S(1)} %all-to-all-done.refs_0_) | copy-start | bytes 786436
  36.1 8.9 %collective-permute-start.1 = (bf16[8,32,512]{2,1,0:T(8,128)(2,1)S(1)}, bf16[8,32,512]{2,1,0:T(8,128)(2,1)S(1)}, u32[]{:S(2)}, u32[]{:S(2)}) collective-permute-start(bf16[8,32,512]{2,1,0:T(8,128)(2,1)S(1)} %all-to-all-done.refs_0_), channel_id=1, source_target_pairs={{0,64},{64,0},{128,192},{192,128},{256,320},{320,256},{384,448},{4... | collective-permute-start | bytes 786440 | tf_op jit(solution)/shard_map/ppermute | solution.py:295
  39.2 8.5 %collective-permute-start.2 = (bf16[8,32,512]{2,1,0:T(8,128)(2,1)S(1)}, bf16[8,32,512]{2,1,0:T(8,128)(2,1)S(1)}, u32[]{:S(2)}, u32[]{:S(2)}) collective-permute-start(bf16[8,32,512]{2,1,0:T(8,128)(2,1)S(1)} %all-to-all-done.refs_0_), channel_id=1, source_target_pairs={{0,320},{64,256},{128,448},{192,384},{256,64},{320,0},{384,192},{4... | collective-permute-start | bytes 786440 | tf_op jit(solution)/shard_map/ppermute | solution.py:295
  43.0 10.0 %collective-permute-start = (bf16[8,32,512]{2,1,0:T(8,128)(2,1)S(1)}, bf16[8,32,512]{2,1,0:T(8,128)(2,1)S(1)}, u32[]{:S(2)}, u32[]{:S(2)}) collective-permute-start(bf16[8,32,512]{2,1,0:T(8,128)(2,1)S(1)} %all-to-all-done.refs_0_), channel_id=1, source_target_pairs={{0,256},{64,320},{128,384},{192,448},{256,0},{320,64},{384,128},{4... | collective-permute-start | bytes 786440 | tf_op jit(solution)/shard_map/ppermute | solution.py:295
  44.9 18.1 %copy-start.5 = (bf16[8,32,512]{2,1,0:T(8,128)(2,1)}, bf16[8,32,512]{2,1,0:T(8,128)(2,1)S(1)}, u32[]{:S(2)}) copy-start(bf16[8,32,512]{2,1,0:T(8,128)(2,1)S(1)} %collective-permute-done.1.refs_2_) | copy-start | bytes 786436
  47.7 5.3 %copy-start.6 = (bf16[8,32,512]{2,1,0:T(8,128)(2,1)}, bf16[8,32,512]{2,1,0:T(8,128)(2,1)S(1)}, u32[]{:S(2)}) copy-start(bf16[8,32,512]{2,1,0:T(8,128)(2,1)S(1)} %collective-permute-done.2.refs_3_) | copy-start | bytes 786436
  52.9 0.7 copy-start.7
  53.8 9.2 %collective-permute-start.3 = (bf16[4,8,32,512]{3,2,1,0:T(8,128)(2,1)S(1)}, bf16[4,8,32,512]{3,2,1,0:T(8,128)(2,1)S(1)}, u32[]{:S(2)}, u32[]{:S(2)}) collective-permute-start(bf16[4,8,32,512]{3,2,1,0:T(8,128)(2,1)S(1)} %pad_maximum_fusion), channel_id=1, source_target_pairs={{0,32},{32,0},{1,33},{33,1},{2,34},{34,2},{3,35},{35,3},{4,36},{36... | collective-permute-start | bytes 3145736 | tf_op jit(solution)/shard_map/ppermute | solution.py:297
  63.0 4.8 %copy-start.1 = (bf16[896,512]{1,0:T(8,128)(2,1)S(1)}, bf16[896,512]{1,0:T(8,128)(2,1)}, u32[]{:S(2)}) copy-start(bf16[896,512]{1,0:T(8,128)(2,1)} %shard_map.67.weight_ref) | copy-start | bytes 2752516
  63.0 4.8 %copy-start.2 = (s32[4]{0:T(128)S(1)}, s32[4]{0:T(128)}, u32[]{:S(2)}) copy-start(s32[4]{0:T(128)} %pad_add_fusion.1.place_ref) | copy-start | bytes 52
  63.0 1.0 copy-start.4
  67.8 7.7 %copy-start = (bf16[8,256,512]{2,1,0:T(8,128)(2,1)S(1)}, bf16[8,256,512]{2,1,0:T(8,128)(2,1)}, u32[]{:S(2)}) copy-start(bf16[8,256,512]{2,1,0:T(8,128)(2,1)} %shard_map.68.cot_ref) | copy-start | bytes 6291460
  72.9 6.7 %collective-permute-start.4 = (bf16[8,8,16,512]{3,2,1,0:T(8,128)(2,1)S(1)}, bf16[8,8,16,512]{3,2,1,0:T(8,128)(2,1)S(1)}, u32[]{:S(2)}, u32[]{:S(2)}) collective-permute-start(bf16[8,8,16,512]{3,2,1,0:T(8,128)(2,1)S(1)} %get-tuple-element.35), channel_id=1, source_target_pairs={{0,32},{32,0},{1,33},{33,1},{2,34},{34,2},{3,35},{35,3},{4,36},{36... | collective-permute-start | bytes 3145736 | tf_op jit(solution)/shard_map/ppermute | solution.py:302
  81.1 20.1 %all-to-all-start.1 = ((bf16[8,8,16,512]{3,2,1,0:T(8,128)(2,1)}), bf16[8,8,16,512]{3,2,1,0:T(8,128)(2,1)S(1)}, u32[]{:S(2)}, u32[]{:S(2)}) async-start(bf16[8,8,16,512]{3,2,1,0:T(8,128)(2,1)} %add_convert_fusion), calls=%async_computation.1 | async-start | bytes 2097152 | tf_op jit(solution)/shard_map/all_to_all | solution.py:311
  86.1 29.5 %collective-permute-start.5 = (bf16[128,896]{1,0:T(8,128)(2,1)S(1)}, bf16[128,896]{1,0:T(8,128)(2,1)S(1)}, u32[]{:S(2)}, u32[]{:S(2)}) collective-permute-start(bf16[128,896]{1,0:T(8,128)(2,1)S(1)} %get-tuple-element.49), channel_id=1, source_target_pairs={{0,16},{8,24},{16,0},{24,8},{1,17},{9,25},{17,1},{25,9},{2,18},{10... | collective-permute-start | bytes 688136 | tf_op jit(solution)/shard_map/ppermute | solution.py:309
  93.2 28.9 %collective-permute-start.6 = (bf16[128,896]{1,0:T(8,128)(2,1)S(1)}, bf16[128,896]{1,0:T(8,128)(2,1)S(1)}, u32[]{:S(2)}, u32[]{:S(2)}) collective-permute-start(bf16[128,896]{1,0:T(8,128)(2,1)S(1)} %get-tuple-element.50), channel_id=1, source_target_pairs={{0,8},{8,16},{16,24},{24,0},{1,9},{9,17},{17,25},{25,1},{2,10},{10... | collective-permute-start | bytes 688136 | tf_op jit(solution)/shard_map/ppermute | solution.py:309
  95.9 26.1 %collective-permute-start.7 = (bf16[128,896]{1,0:T(8,128)(2,1)S(1)}, bf16[128,896]{1,0:T(8,128)(2,1)S(1)}, u32[]{:S(2)}, u32[]{:S(2)}) collective-permute-start(bf16[128,896]{1,0:T(8,128)(2,1)S(1)} %get-tuple-element.51), channel_id=1, source_target_pairs={{0,24},{8,0},{16,8},{24,16},{1,25},{9,1},{17,9},{25,17},{2,26},{10... | collective-permute-start | bytes 688136 | tf_op jit(solution)/shard_map/ppermute | solution.py:309
  102.0 21.2 %all-to-all-start.2 = ((bf16[8,16,512]{2,1,0:T(8,128)(2,1)}), bf16[8,16,512]{2,1,0:T(8,128)(2,1)S(1)}, u32[]{:S(2)}, u32[]{:S(2)}) async-start(bf16[8,16,512]{2,1,0:T(8,128)(2,1)} %reduce_sum.12), calls=%async_computation.2 | async-start | bytes 262144 | tf_op jit(solution)/shard_map/all_to_all | solution.py:313
Sparse Core Ops, SparseCore 0:
  10.1 57.6 all-gather.5
  69.9 38.6 all-gather.7

commit v5 on v4

--- a/solution.py
+++ b/solution.py
@@ -294,6 +294,7 @@
         pairs = [(z * X + i, (z ^ flip_z) * X + (i ^ flip_x)) for z in range(Z_LO) for i in range(X)]
         parts.append(lax.ppermute(mine, ("z_lo", "x"), pairs))
     weight = near_weight(near)
+    weight, *parts = lax.optimization_barrier((weight, *parts))
     other = lax.ppermute(jnp.stack(parts), "core", ring(CORE, 1))
     cot = assemble(place, parts, other)
     hid, weight, cot = lax.optimization_barrier((hid, weight, cot))

time: 133 us -> 132 us (level)
  starting transfers between devices: 49.3 us -> 50.8 us
    ppermute x3, waiting for transfers between devices: 7.99 us -> 3.26 us  [per_device(): parts.append(lax.ppermute(mine, ('z_lo', 'x'), pairs))]
    ppermute x1, starting transfers between devices: 5.37 us -> 7.78 us  [per_device(): other = lax.ppermute(jnp.stack(parts), 'core', ring(CORE, 1))]
    ppermute x1, waiting for transfers between devices: 0.01 us -> 1.65 us  [per_device(): other = lax.ppermute(jnp.stack(parts), 'core', ring(CORE, 1))]
    all_gather x1, waiting for transfers between devices: 0.26 us -> 1.62 us  [per_device(): hid = lax.all_gather(hidden, 'y')]
where the time goes in v5:
time: 132 us; the launch traced here: 131 us
  starting transfers between devices  50.8 us (38%)
  Pallas kernels  23 us (17%)
  blocking collectives  18.3 us (14%)
  waiting for transfers between devices  16.5 us (12%)
  between operations  14.3 us (11%)
  local copies, waits for them, and re-layouts  4.87 us (4%)
  other arithmetic  3.17 us (2%)
    all_gather x1, blocking collectives, per_device(): near = lax.all_gather(pack_block(packed_codes, block_scales), 'z_hi')  18.3 us
    ppermute x3, starting transfers between devices, per_device(): lax.ppermute(others[d - 1], 'z_hi', ring(Z_HI, d))  14.5 us
    ppermute x3, starting transfers between devices, per_device(): parts.append(lax.ppermute(mine, ('z_lo', 'x'), pairs))  8.85 us
    ppermute x1, starting transfers between devices, per_device(): other = lax.ppermute(jnp.stack(parts), 'core', ring(CORE, 1))  7.78 us
    all_to_all x1, starting transfers between devices, per_device(): mine = lax.all_to_all(mine, 'y', 0, 0)  7.65 us
    pallas_call x1, Pallas kernels, grad_hidden_of(): pl.pallas_call(grad_hidden_kernel, in_specs=[pl.BlockSpec(memory_space=pl...  7.04 us
    ppermute x3, waiting for transfers between devices, per_device(): lax.ppermute(others[d - 1], 'z_hi', ring(Z_HI, d))  6.45 us
    pallas_call x1, Pallas kernels, ring_outputs(): pl.pallas_call(outputs_kernel, grid_spec=pltpu.PrefetchScalarGridSpec(num...  5.06 us
  transfers between devices with their start and end apart: 13, of which 6 were waited for; matrix products, arithmetic and copies ran while one was open for 5% of the time, Pallas kernels for 18%

profile of v5, /device:TPU:1, one launch (start us, length us, event | category | flops | bytes accessed | tf_op | source)
XLA Modules:
  0.0 130.8 jit_solution(11562425569346931273)
XLA Ops:
  7.2 0.7 all-gather.6.cloned.1.call-update
  7.9 1.0 dynamic-slice_bitcast_fusion
  9.1 0.8 reshape.19
  9.9 7.7 %all-to-all-start = ((bf16[8,32,512]{2,1,0:T(8,128)(2,1)}), bf16[8,32,512]{2,1,0:T(8,128)(2,1)S(1)}, u32[]{:S(2)}, u32[]{:S(2)}) async-start(bf16[8,32,512]{2,1,0:T(8,128)(2,1)} %reshape.19), calls=%async_computation | async-start | bytes 524288 | tf_op jit(solution)/shard_map/all_to_all | solution.py:290
  17.8 18.3 %all-gather.1 = s32[480,128]{1,0:T(8,128)} all-gather(s32[120,128]{1,0:T(8,128)S(1)} %pad_add_fusion), channel_id=3, replica_groups=mesh['z_lo'=2,'x'=4,'core'=2,'z_hi'=4,'y'=8] {'z_hi'}, dimensions={0}, use_global_device_ids=true | all-gather | bytes 307200 | tf_op jit(solution)/shard_map/all_gather | solution.py:285
  36.1 3.8 %collective-permute-start = (bf16[8,32,512]{2,1,0:T(8,128)(2,1)S(1)}, bf16[8,32,512]{2,1,0:T(8,128)(2,1)S(1)}, u32[]{:S(2)}, u32[]{:S(2)}) collective-permute-start(bf16[8,32,512]{2,1,0:T(8,128)(2,1)S(1)} %all-to-all-done.refs_0_), channel_id=1, source_target_pairs={{0,256},{64,320},{128,384},{192,448},{256,0},{320,64},{384,128},{4... | collective-permute-start | bytes 786440 | tf_op jit(solution)/shard_map/ppermute | solution.py:295
  39.9 3.1 %collective-permute-start.1 = (bf16[8,32,512]{2,1,0:T(8,128)(2,1)S(1)}, bf16[8,32,512]{2,1,0:T(8,128)(2,1)S(1)}, u32[]{:S(2)}, u32[]{:S(2)}) collective-permute-start(bf16[8,32,512]{2,1,0:T(8,128)(2,1)S(1)} %all-to-all-done.refs_0_), channel_id=1, source_target_pairs={{0,64},{64,0},{128,192},{192,128},{256,320},{320,256},{384,448},{4... | collective-permute-start | bytes 786440 | tf_op jit(solution)/shard_map/ppermute | solution.py:295
  43.0 1.9 %collective-permute-start.2 = (bf16[8,32,512]{2,1,0:T(8,128)(2,1)S(1)}, bf16[8,32,512]{2,1,0:T(8,128)(2,1)S(1)}, u32[]{:S(2)}, u32[]{:S(2)}) collective-permute-start(bf16[8,32,512]{2,1,0:T(8,128)(2,1)S(1)} %all-to-all-done.refs_0_), channel_id=1, source_target_pairs={{0,320},{64,256},{128,448},{192,384},{256,64},{320,0},{384,192},{4... | collective-permute-start | bytes 786440 | tf_op jit(solution)/shard_map/ppermute | solution.py:295
  44.9 3.3 %shard_map.67.weight_ref = bf16[896,512]{1,0:T(8,128)(2,1)} custom-call(s32[4,120,128]{2,1,0:T(8,128)} %bitcast.28), custom_call_target="tpu_custom_call" | custom-call | flops 2000000 | bytes 1200000 | tf_op jit(solution)/shard_map/pallas_call | solution.py:54
  48.2 3.3 %collective-permute-done.2.refs_3_ = bf16[8,32,512]{2,1,0:T(8,128)(2,1)S(1)} collective-permute-done((bf16[8,32,512]{2,1,0:T(8,128)(2,1)S(1)}, bf16[8,32,512]{2,1,0:T(8,128)(2,1)S(1)}, u32[]{:S(2)}, u32[]{:S(2)}) %collective-permute-start.2) | collective-permute-done | bytes 262176 | tf_op jit(solution)/shard_map/ppermute | solution.py:295
  51.6 7.8 %collective-permute-start.3 = (bf16[4,8,32,512]{3,2,1,0:T(8,128)(2,1)S(1)}, bf16[4,8,32,512]{3,2,1,0:T(8,128)(2,1)S(1)}, u32[]{:S(2)}, u32[]{:S(2)}) collective-permute-start(bf16[4,8,32,512]{3,2,1,0:T(8,128)(2,1)S(1)} %pad_maximum_fusion), channel_id=1, source_target_pairs={{0,32},{32,0},{1,33},{33,1},{2,34},{34,2},{3,35},{35,3},{4,36},{36... | collective-permute-start | bytes 3145736 | tf_op jit(solution)/shard_map/ppermute | solution.py:298
  59.4 0.6 pad_add_fusion.1.place_ref
  60.0 1.7 %collective-permute-done.3.refs_4_ = bf16[4,8,32,512]{3,2,1,0:T(8,128)(2,1)S(1)} collective-permute-done((bf16[4,8,32,512]{3,2,1,0:T(8,128)(2,1)S(1)}, bf16[4,8,32,512]{3,2,1,0:T(8,128)(2,1)S(1)}, u32[]{:S(2)}, u32[]{:S(2)}) %collective-permute-start.3) | collective-permute-done | bytes 1048608 | tf_op jit(solution)/shard_map/ppermute | solution.py:298
  61.7 1.0 copy-done.4
  62.7 3.5 %shard_map.68.cot_ref = bf16[8,256,512]{2,1,0:T(8,128)(2,1)} custom-call(s32[4]{0:T(128)} %pad_add_fusion.1.place_ref, bf16[8,32,512]{2,1,0:T(8,128)(2,1)} %copy-done.3, bf16[8,32,512]{2,1,0:T(8,128)(2,1)} %copy-done.5, bf16[8,32,512]{2,1,0:T(8,128)(2,1)} %copy-done.6, bf16[8,32,512]{2,1,0:T(8,128)(2,1)} %copy-done.7, bf16[4,8,32,512]{3,2,1,0:T(8,128)(2,1)} %copy-done.4), custom_call_target="tpu_custom_call" | custom-call | bytes 4000000 | tf_op jit(solution)/shard_map/pallas_call | solution.py:82
  66.2 1.6 %all-gather.6.cloned.1.call-done = bf16[2048,896]{1,0:T(8,128)(2,1)} async-done(((bf16[256,896]{1,0:T(8,128)(2,1)}), bf16[2048,896]{1,0:T(8,128)(2,1)}) %all-gather.6.cloned.1.call-update) | async-done | bytes 3670032 | tf_op jit(solution)/shard_map/all_gather | solution.py:284
  67.8 5.1 %shard_map.69 = (bf16[8,8,16,512]{3,2,1,0:T(8,128)(2,1)S(1)}, bf16[8,8,16,512]{3,2,1,0:T(8,128)(2,1)S(1)}) custom-call(s32[4]{0:T(128)S(1)} %copy-done.2, bf16[8,256,896]{2,1,0:T(8,128)(2,1)} %bitcast.37, bf16[896,512]{1,0:T(8,128)(2,1)S(1)} %copy-done.1), custom_call_target="tpu_custom_call" | custom-call | flops 1879048192 | bytes 7000000 | tf_op jit(solution)/shard_map/pallas_call | solution.py:134
  72.9 2.6 %collective-permute-start.4 = (bf16[8,8,16,512]{3,2,1,0:T(8,128)(2,1)S(1)}, bf16[8,8,16,512]{3,2,1,0:T(8,128)(2,1)S(1)}, u32[]{:S(2)}, u32[]{:S(2)}) collective-permute-start(bf16[8,8,16,512]{3,2,1,0:T(8,128)(2,1)S(1)} %get-tuple-element.45), channel_id=1, source_target_pairs={{0,32},{32,0},{1,33},{33,1},{2,34},{34,2},{3,35},{35,3},{4,36},{36... | collective-permute-start | bytes 3145736 | tf_op jit(solution)/shard_map/ppermute | solution.py:303
  75.5 4.1 %shard_map.70 = (bf16[128,896]{1,0:T(8,128)(2,1)S(1)}, bf16[128,896]{1,0:T(8,128)(2,1)S(1)}, bf16[128,896]{1,0:T(8,128)(2,1)S(1)}, bf16[128,896]{1,0:T(8,128)(2,1)S(1)}) custom-call(bf16[8,256,896]{2,1,0:T(8,128)(2,1)} %bitcast.38, bf16[8,256,512]{2,1,0:T(8,128)(2,1)S(1)} %copy-done), custom_call_target="tpu_custom_call" | custom-call | flops 1879048192 | bytes 7000000 | tf_op jit(solution)/shard_map/pallas_call | solution.py:187
  79.6 1.4 %add_convert_fusion = bf16[8,8,16,512]{3,2,1,0:T(8,128)(2,1)} fusion(bf16[8,8,16,512]{3,2,1,0:T(8,128)(2,1)S(1)} %collective-permute-done.4, bf16[8,8,16,512]{3,2,1,0:T(8,128)(2,1)S(1)} %get-tuple-element.44), kind=kLoop, calls=%fused_computation | loop fusion | flops 2097152 | bytes 3145728 | tf_op jit(solution)/shard_map/convert_element_type | solution.py:307
  81.1 5.1 %all-to-all-start.1 = ((bf16[8,8,16,512]{3,2,1,0:T(8,128)(2,1)}), bf16[8,8,16,512]{3,2,1,0:T(8,128)(2,1)S(1)}, u32[]{:S(2)}, u32[]{:S(2)}) async-start(bf16[8,8,16,512]{3,2,1,0:T(8,128)(2,1)} %add_convert_fusion), calls=%async_computation.1 | async-start | bytes 2097152 | tf_op jit(solution)/shard_map/all_to_all | solution.py:312
  86.1 7.1 %collective-permute-start.5 = (bf16[128,896]{1,0:T(8,128)(2,1)S(1)}, bf16[128,896]{1,0:T(8,128)(2,1)S(1)}, u32[]{:S(2)}, u32[]{:S(2)}) collective-permute-start(bf16[128,896]{1,0:T(8,128)(2,1)S(1)} %get-tuple-element.59), channel_id=1, source_target_pairs={{0,16},{8,24},{16,0},{24,8},{1,17},{9,25},{17,1},{25,9},{2,18},{10... | collective-permute-start | bytes 688136 | tf_op jit(solution)/shard_map/ppermute | solution.py:310
  93.2 2.7 %collective-permute-start.6 = (bf16[128,896]{1,0:T(8,128)(2,1)S(1)}, bf16[128,896]{1,0:T(8,128)(2,1)S(1)}, u32[]{:S(2)}, u32[]{:S(2)}) collective-permute-start(bf16[128,896]{1,0:T(8,128)(2,1)S(1)} %get-tuple-element.60), channel_id=1, source_target_pairs={{0,8},{8,16},{16,24},{24,0},{1,9},{9,17},{17,25},{25,1},{2,10},{10... | collective-permute-start | bytes 688136 | tf_op jit(solution)/shard_map/ppermute | solution.py:310
  95.9 4.7 %collective-permute-start.7 = (bf16[128,896]{1,0:T(8,128)(2,1)S(1)}, bf16[128,896]{1,0:T(8,128)(2,1)S(1)}, u32[]{:S(2)}, u32[]{:S(2)}) collective-permute-start(bf16[128,896]{1,0:T(8,128)(2,1)S(1)} %get-tuple-element.61), channel_id=1, source_target_pairs={{0,24},{8,0},{16,8},{24,16},{1,25},{9,1},{17,9},{25,17},{2,26},{10... | collective-permute-start | bytes 688136 | tf_op jit(solution)/shard_map/ppermute | solution.py:310
  100.6 0.5 all-to-all-done.1
  101.1 0.8 reduce_sum.12
  102.0 4.3 %all-to-all-start.2 = ((bf16[8,16,512]{2,1,0:T(8,128)(2,1)}), bf16[8,16,512]{2,1,0:T(8,128)(2,1)S(1)}, u32[]{:S(2)}, u32[]{:S(2)}) async-start(bf16[8,16,512]{2,1,0:T(8,128)(2,1)} %reduce_sum.12), calls=%async_computation.2 | async-start | bytes 262144 | tf_op jit(solution)/shard_map/all_to_all | solution.py:314
  106.3 2.3 %all-gather.8.cloned.1.call-done = s32[32,120,128]{2,1,0:T(8,128)} async-done(((s32[4,120,128]{2,1,0:T(8,128)}), s32[32,120,128]{2,1,0:T(8,128)}) %all-gather.8.cloned.1.call-update) | async-done | bytes 1966096 | tf_op jit(solution)/shard_map/all_gather | solution.py:317
  108.6 7.0 %shard_map.71 = bf16[256,896]{1,0:T(8,128)(2,1)} custom-call(bf16[256,4096]{1,0:T(8,128)(2,1)} %cot_ref.1, s32[8,4,120,128]{3,2,1,0:T(8,128)} %bitcast.39), custom_call_target="tpu_custom_call" | custom-call | flops 1879048192 | bytes 6000000 | tf_op jit(solution)/shard_map/pallas_call | solution.py:255
  115.6 6.4 %collective-permute-done.6 = bf16[128,896]{1,0:T(8,128)(2,1)S(1)} collective-permute-done((bf16[128,896]{1,0:T(8,128)(2,1)S(1)}, bf16[128,896]{1,0:T(8,128)(2,1)S(1)}, u32[]{:S(2)}, u32[]{:S(2)}) %collective-permute-start.6) | collective-permute-done | bytes 229408 | tf_op jit(solution)/shard_map/ppermute | solution.py:310
  122.2 1.0 copy.15
  123.3 0.7 copy.19
  (40 shorter events, 0.8 us)
Async XLA Ops:
  7.2 10.4 %copy-start.9 = (f32[7,1]{0,1:T(1,128)S(1)}, f32[7,1]{0,1:T(1,128)}, u32[]{:S(2)}) copy-start(f32[7,1]{0,1:T(1,128)} %param.7) | copy-start | bytes 88
  7.2 10.5 %copy-start.8 = (s32[224,128]{1,0:T(8,128)S(1)}, s32[224,128]{1,0:T(8,128)}, u32[]{:S(2)}) copy-start(s32[224,128]{1,0:T(8,128)} %param.6) | copy-start | bytes 344068
  7.2 60.7 %all-gather.6.cloned.1.call-start = ((), (), s32[]{:S(2)}) async-start(), calls=%async_computation.3 | async-start | bytes 4128768 | tf_op jit(solution)/shard_map/all_gather | solution.py:284
  9.9 26.2 %all-to-all-start = ((bf16[8,32,512]{2,1,0:T(8,128)(2,1)}), bf16[8,32,512]{2,1,0:T(8,128)(2,1)S(1)}, u32[]{:S(2)}, u32[]{:S(2)}) async-start(bf16[8,32,512]{2,1,0:T(8,128)(2,1)} %reshape.19), calls=%async_computation | async-start | bytes 524288 | tf_op jit(solution)/shard_map/all_to_all | solution.py:290
  17.5 91.0 %all-gather.8.cloned.1.call-start = ((), (), s32[]{:S(2)}) async-start(), calls=%async_computation.4 | async-start | bytes 2211840 | tf_op jit(solution)/shard_map/all_gather | solution.py:317
  36.1 25.6 %copy-start.3 = (bf16[8,32,512]{2,1,0:T(8,128)(2,1)}, bf16[8,32,512]{2,1,0:T(8,128)(2,1)S(1)}, u32[]{:S(2)}) copy-start(bf16[8,32,512]{2,1,0:T(8,128)(2,1)S(1)} %all-to-all-done.refs_0_) | copy-start | bytes 786436
  36.1 12.1 %collective-permute-start = (bf16[8,32,512]{2,1,0:T(8,128)(2,1)S(1)}, bf16[8,32,512]{2,1,0:T(8,128)(2,1)S(1)}, u32[]{:S(2)}, u32[]{:S(2)}) collective-permute-start(bf16[8,32,512]{2,1,0:T(8,128)(2,1)S(1)} %all-to-all-done.refs_0_), channel_id=1, source_target_pairs={{0,256},{64,320},{128,384},{192,448},{256,0},{320,64},{384,128},{4... | collective-permute-start | bytes 786440 | tf_op jit(solution)/shard_map/ppermute | solution.py:295
  39.9 8.3 %collective-permute-start.1 = (bf16[8,32,512]{2,1,0:T(8,128)(2,1)S(1)}, bf16[8,32,512]{2,1,0:T(8,128)(2,1)S(1)}, u32[]{:S(2)}, u32[]{:S(2)}) collective-permute-start(bf16[8,32,512]{2,1,0:T(8,128)(2,1)S(1)} %all-to-all-done.refs_0_), channel_id=1, source_target_pairs={{0,64},{64,0},{128,192},{192,128},{256,320},{320,256},{384,448},{4... | collective-permute-start | bytes 786440 | tf_op jit(solution)/shard_map/ppermute | solution.py:295
  43.0 8.5 %collective-permute-start.2 = (bf16[8,32,512]{2,1,0:T(8,128)(2,1)S(1)}, bf16[8,32,512]{2,1,0:T(8,128)(2,1)S(1)}, u32[]{:S(2)}, u32[]{:S(2)}) collective-permute-start(bf16[8,32,512]{2,1,0:T(8,128)(2,1)S(1)} %all-to-all-done.refs_0_), channel_id=1, source_target_pairs={{0,320},{64,256},{128,448},{192,384},{256,64},{320,0},{384,192},{4... | collective-permute-start | bytes 786440 | tf_op jit(solution)/shard_map/ppermute | solution.py:295
  48.2 13.5 %copy-start.5 = (bf16[8,32,512]{2,1,0:T(8,128)(2,1)}, bf16[8,32,512]{2,1,0:T(8,128)(2,1)S(1)}, u32[]{:S(2)}) copy-start(bf16[8,32,512]{2,1,0:T(8,128)(2,1)S(1)} %collective-permute-done.refs_1_) | copy-start | bytes 786436
  48.2 11.2 %copy-start.6 = (bf16[8,32,512]{2,1,0:T(8,128)(2,1)}, bf16[8,32,512]{2,1,0:T(8,128)(2,1)S(1)}, u32[]{:S(2)}) copy-start(bf16[8,32,512]{2,1,0:T(8,128)(2,1)S(1)} %collective-permute-done.1.refs_2_) | copy-start | bytes 786436
  51.5 8.0 %copy-start.7 = (bf16[8,32,512]{2,1,0:T(8,128)(2,1)}, bf16[8,32,512]{2,1,0:T(8,128)(2,1)S(1)}, u32[]{:S(2)}) copy-start(bf16[8,32,512]{2,1,0:T(8,128)(2,1)S(1)} %collective-permute-done.2.refs_3_) | copy-start | bytes 786436
  51.6 10.1 %collective-permute-start.3 = (bf16[4,8,32,512]{3,2,1,0:T(8,128)(2,1)S(1)}, bf16[4,8,32,512]{3,2,1,0:T(8,128)(2,1)S(1)}, u32[]{:S(2)}, u32[]{:S(2)}) collective-permute-start(bf16[4,8,32,512]{3,2,1,0:T(8,128)(2,1)S(1)} %pad_maximum_fusion), channel_id=1, source_target_pairs={{0,32},{32,0},{1,33},{33,1},{2,34},{34,2},{3,35},{35,3},{4,36},{36... | collective-permute-start | bytes 3145736 | tf_op jit(solution)/shard_map/ppermute | solution.py:298
  60.0 7.8 %copy-start.1 = (bf16[896,512]{1,0:T(8,128)(2,1)S(1)}, bf16[896,512]{1,0:T(8,128)(2,1)}, u32[]{:S(2)}) copy-start(bf16[896,512]{1,0:T(8,128)(2,1)} %shard_map.67.weight_ref) | copy-start | bytes 2752516
  60.0 7.8 %copy-start.2 = (s32[4]{0:T(128)S(1)}, s32[4]{0:T(128)}, u32[]{:S(2)}) copy-start(s32[4]{0:T(128)} %pad_add_fusion.1.place_ref) | copy-start | bytes 52
  61.7 1.0 copy-start.4
  67.8 7.7 %copy-start = (bf16[8,256,512]{2,1,0:T(8,128)(2,1)S(1)}, bf16[8,256,512]{2,1,0:T(8,128)(2,1)}, u32[]{:S(2)}) copy-start(bf16[8,256,512]{2,1,0:T(8,128)(2,1)} %shard_map.68.cot_ref) | copy-start | bytes 6291460
  72.9 6.7 %collective-permute-start.4 = (bf16[8,8,16,512]{3,2,1,0:T(8,128)(2,1)S(1)}, bf16[8,8,16,512]{3,2,1,0:T(8,128)(2,1)S(1)}, u32[]{:S(2)}, u32[]{:S(2)}) collective-permute-start(bf16[8,8,16,512]{3,2,1,0:T(8,128)(2,1)S(1)} %get-tuple-element.45), channel_id=1, source_target_pairs={{0,32},{32,0},{1,33},{33,1},{2,34},{34,2},{3,35},{35,3},{4,36},{36... | collective-permute-start | bytes 3145736 | tf_op jit(solution)/shard_map/ppermute | solution.py:303
  81.1 20.1 %all-to-all-start.1 = ((bf16[8,8,16,512]{3,2,1,0:T(8,128)(2,1)}), bf16[8,8,16,512]{3,2,1,0:T(8,128)(2,1)S(1)}, u32[]{:S(2)}, u32[]{:S(2)}) async-start(bf16[8,8,16,512]{3,2,1,0:T(8,128)(2,1)} %add_convert_fusion), calls=%async_computation.1 | async-start | bytes 2097152 | tf_op jit(solution)/shard_map/all_to_all | solution.py:312
  86.1 29.5 %collective-permute-start.5 = (bf16[128,896]{1,0:T(8,128)(2,1)S(1)}, bf16[128,896]{1,0:T(8,128)(2,1)S(1)}, u32[]{:S(2)}, u32[]{:S(2)}) collective-permute-start(bf16[128,896]{1,0:T(8,128)(2,1)S(1)} %get-tuple-element.59), channel_id=1, source_target_pairs={{0,16},{8,24},{16,0},{24,8},{1,17},{9,25},{17,1},{25,9},{2,18},{10... | collective-permute-start | bytes 688136 | tf_op jit(solution)/shard_map/ppermute | solution.py:310
  93.2 28.9 %collective-permute-start.6 = (bf16[128,896]{1,0:T(8,128)(2,1)S(1)}, bf16[128,896]{1,0:T(8,128)(2,1)S(1)}, u32[]{:S(2)}, u32[]{:S(2)}) collective-permute-start(bf16[128,896]{1,0:T(8,128)(2,1)S(1)} %get-tuple-element.60), channel_id=1, source_target_pairs={{0,8},{8,16},{16,24},{24,0},{1,9},{9,17},{17,25},{25,1},{2,10},{10... | collective-permute-start | bytes 688136 | tf_op jit(solution)/shard_map/ppermute | solution.py:310
  95.9 26.1 %collective-permute-start.7 = (bf16[128,896]{1,0:T(8,128)(2,1)S(1)}, bf16[128,896]{1,0:T(8,128)(2,1)S(1)}, u32[]{:S(2)}, u32[]{:S(2)}) collective-permute-start(bf16[128,896]{1,0:T(8,128)(2,1)S(1)} %get-tuple-element.61), channel_id=1, source_target_pairs={{0,24},{8,0},{16,8},{24,16},{1,25},{9,1},{17,9},{25,17},{2,26},{10... | collective-permute-start | bytes 688136 | tf_op jit(solution)/shard_map/ppermute | solution.py:310
  102.0 21.2 %all-to-all-start.2 = ((bf16[8,16,512]{2,1,0:T(8,128)(2,1)}), bf16[8,16,512]{2,1,0:T(8,128)(2,1)S(1)}, u32[]{:S(2)}, u32[]{:S(2)}) async-start(bf16[8,16,512]{2,1,0:T(8,128)(2,1)} %reduce_sum.12), calls=%async_computation.2 | async-start | bytes 262144 | tf_op jit(solution)/shard_map/all_to_all | solution.py:314
Sparse Core Ops, SparseCore 0:
  10.1 57.6 all-gather.5
  69.9 38.6 all-gather.7

commit v6 on v5

--- a/solution.py
+++ b/solution.py
@@ -290,9 +290,10 @@
     mine = lax.all_to_all(mine, "y", 0, 0)
     mine, near = lax.optimization_barrier((mine, near))
     parts = [mine]
-    for flip_z, flip_x in ((1, 0), (0, 1), (1, 1)):
+    for flip_z, flip_x in ((1, 1), (1, 0), (0, 1)):
         pairs = [(z * X + i, (z ^ flip_z) * X + (i ^ flip_x)) for z in range(Z_LO) for i in range(X)]
         parts.append(lax.ppermute(mine, ("z_lo", "x"), pairs))
+    parts.append(parts.pop(1))
     weight = near_weight(near)
     weight, *parts = lax.optimization_barrier((weight, *parts))
     other = lax.ppermute(jnp.stack(parts), "core", ring(CORE, 1))

time: 132 us -> 132 us (level)
  no operation moved by 1% of the time
where the time goes in v6:
time: 132 us; the launch traced here: 131 us
  starting transfers between devices  50.8 us (38%)
  Pallas kernels  23 us (17%)
  blocking collectives  18.3 us (14%)
  waiting for transfers between devices  16.5 us (12%)
  between operations  14.3 us (11%)
  local copies, waits for them, and re-layouts  4.87 us (4%)
  other arithmetic  3.17 us (2%)
    all_gather x1, blocking collectives, per_device(): near = lax.all_gather(pack_block(packed_codes, block_scales), 'z_hi')  18.3 us
    ppermute x3, starting transfers between devices, per_device(): lax.ppermute(others[d - 1], 'z_hi', ring(Z_HI, d))  14.5 us
    ppermute x3, starting transfers between devices, per_device(): parts.append(lax.ppermute(mine, ('z_lo', 'x'), pairs))  8.85 us
    ppermute x1, starting transfers between devices, per_device(): other = lax.ppermute(jnp.stack(parts), 'core', ring(CORE, 1))  7.78 us
    all_to_all x1, starting transfers between devices, per_device(): mine = lax.all_to_all(mine, 'y', 0, 0)  7.65 us
    pallas_call x1, Pallas kernels, grad_hidden_of(): pl.pallas_call(grad_hidden_kernel, in_specs=[pl.BlockSpec(memory_space=pl...  7.04 us
    ppermute x3, waiting for transfers between devices, per_device(): lax.ppermute(others[d - 1], 'z_hi', ring(Z_HI, d))  6.45 us
    pallas_call x1, Pallas kernels, ring_outputs(): pl.pallas_call(outputs_kernel, grid_spec=pltpu.PrefetchScalarGridSpec(num...  5.06 us
  transfers between devices with their start and end apart: 13, of which 6 were waited for; matrix products, arithmetic and copies ran while one was open for 5% of the time, Pallas kernels for 18%

profile of v6, /device:TPU:1, one launch (start us, length us, event | category | flops | bytes accessed | tf_op | source)
XLA Modules:
  0.0 130.8 jit_solution(11562425569346931273)
XLA Ops:
  7.2 0.7 all-gather.6.cloned.1.call-update
  7.9 1.0 dynamic-slice_bitcast_fusion
  9.1 0.8 reshape.19
  9.9 7.7 %all-to-all-start = ((bf16[8,32,512]{2,1,0:T(8,128)(2,1)}), bf16[8,32,512]{2,1,0:T(8,128)(2,1)S(1)}, u32[]{:S(2)}, u32[]{:S(2)}) async-start(bf16[8,32,512]{2,1,0:T(8,128)(2,1)} %reshape.19), calls=%async_computation | async-start | bytes 524288 | tf_op jit(solution)/shard_map/all_to_all | solution.py:290
  17.8 18.3 %all-gather.1 = s32[480,128]{1,0:T(8,128)} all-gather(s32[120,128]{1,0:T(8,128)S(1)} %pad_add_fusion), channel_id=3, replica_groups=mesh['z_lo'=2,'x'=4,'core'=2,'z_hi'=4,'y'=8] {'z_hi'}, dimensions={0}, use_global_device_ids=true | all-gather | bytes 307200 | tf_op jit(solution)/shard_map/all_gather | solution.py:285
  36.1 3.8 %collective-permute-start = (bf16[8,32,512]{2,1,0:T(8,128)(2,1)S(1)}, bf16[8,32,512]{2,1,0:T(8,128)(2,1)S(1)}, u32[]{:S(2)}, u32[]{:S(2)}) collective-permute-start(bf16[8,32,512]{2,1,0:T(8,128)(2,1)S(1)} %all-to-all-done.refs_0_), channel_id=1, source_target_pairs={{0,256},{64,320},{128,384},{192,448},{256,0},{320,64},{384,128},{4... | collective-permute-start | bytes 786440 | tf_op jit(solution)/shard_map/ppermute | solution.py:295
  39.9 3.1 %collective-permute-start.1 = (bf16[8,32,512]{2,1,0:T(8,128)(2,1)S(1)}, bf16[8,32,512]{2,1,0:T(8,128)(2,1)S(1)}, u32[]{:S(2)}, u32[]{:S(2)}) collective-permute-start(bf16[8,32,512]{2,1,0:T(8,128)(2,1)S(1)} %all-to-all-done.refs_0_), channel_id=1, source_target_pairs={{0,64},{64,0},{128,192},{192,128},{256,320},{320,256},{384,448},{4... | collective-permute-start | bytes 786440 | tf_op jit(solution)/shard_map/ppermute | solution.py:295
  43.0 1.9 %collective-permute-start.2 = (bf16[8,32,512]{2,1,0:T(8,128)(2,1)S(1)}, bf16[8,32,512]{2,1,0:T(8,128)(2,1)S(1)}, u32[]{:S(2)}, u32[]{:S(2)}) collective-permute-start(bf16[8,32,512]{2,1,0:T(8,128)(2,1)S(1)} %all-to-all-done.refs_0_), channel_id=1, source_target_pairs={{0,320},{64,256},{128,448},{192,384},{256,64},{320,0},{384,192},{4... | collective-permute-start | bytes 786440 | tf_op jit(solution)/shard_map/ppermute | solution.py:295
  44.9 3.3 %shard_map.67.weight_ref = bf16[896,512]{1,0:T(8,128)(2,1)} custom-call(s32[4,120,128]{2,1,0:T(8,128)} %bitcast.28), custom_call_target="tpu_custom_call" | custom-call | flops 2000000 | bytes 1200000 | tf_op jit(solution)/shard_map/pallas_call | solution.py:54
  48.2 3.3 %collective-permute-done.2.refs_3_ = bf16[8,32,512]{2,1,0:T(8,128)(2,1)S(1)} collective-permute-done((bf16[8,32,512]{2,1,0:T(8,128)(2,1)S(1)}, bf16[8,32,512]{2,1,0:T(8,128)(2,1)S(1)}, u32[]{:S(2)}, u32[]{:S(2)}) %collective-permute-start.2) | collective-permute-done | bytes 262176 | tf_op jit(solution)/shard_map/ppermute | solution.py:295
  51.6 7.8 %collective-permute-start.3 = (bf16[4,8,32,512]{3,2,1,0:T(8,128)(2,1)S(1)}, bf16[4,8,32,512]{3,2,1,0:T(8,128)(2,1)S(1)}, u32[]{:S(2)}, u32[]{:S(2)}) collective-permute-start(bf16[4,8,32,512]{3,2,1,0:T(8,128)(2,1)S(1)} %pad_maximum_fusion), channel_id=1, source_target_pairs={{0,32},{32,0},{1,33},{33,1},{2,34},{34,2},{3,35},{35,3},{4,36},{36... | collective-permute-start | bytes 3145736 | tf_op jit(solution)/shard_map/ppermute | solution.py:299
  59.4 0.6 pad_add_fusion.1.place_ref
  60.0 1.7 %collective-permute-done.3.refs_4_ = bf16[4,8,32,512]{3,2,1,0:T(8,128)(2,1)S(1)} collective-permute-done((bf16[4,8,32,512]{3,2,1,0:T(8,128)(2,1)S(1)}, bf16[4,8,32,512]{3,2,1,0:T(8,128)(2,1)S(1)}, u32[]{:S(2)}, u32[]{:S(2)}) %collective-permute-start.3) | collective-permute-done | bytes 1048608 | tf_op jit(solution)/shard_map/ppermute | solution.py:299
  61.7 1.0 copy-done.4
  62.7 3.5 %shard_map.68.cot_ref = bf16[8,256,512]{2,1,0:T(8,128)(2,1)} custom-call(s32[4]{0:T(128)} %pad_add_fusion.1.place_ref, bf16[8,32,512]{2,1,0:T(8,128)(2,1)} %copy-done.3, bf16[8,32,512]{2,1,0:T(8,128)(2,1)} %copy-done.5, bf16[8,32,512]{2,1,0:T(8,128)(2,1)} %copy-done.6, bf16[8,32,512]{2,1,0:T(8,128)(2,1)} %copy-done.7, bf16[4,8,32,512]{3,2,1,0:T(8,128)(2,1)} %copy-done.4), custom_call_target="tpu_custom_call" | custom-call | bytes 4000000 | tf_op jit(solution)/shard_map/pallas_call | solution.py:82
  66.2 1.6 %all-gather.6.cloned.1.call-done = bf16[2048,896]{1,0:T(8,128)(2,1)} async-done(((bf16[256,896]{1,0:T(8,128)(2,1)}), bf16[2048,896]{1,0:T(8,128)(2,1)}) %all-gather.6.cloned.1.call-update) | async-done | bytes 3670032 | tf_op jit(solution)/shard_map/all_gather | solution.py:284
  67.8 5.1 %shard_map.69 = (bf16[8,8,16,512]{3,2,1,0:T(8,128)(2,1)S(1)}, bf16[8,8,16,512]{3,2,1,0:T(8,128)(2,1)S(1)}) custom-call(s32[4]{0:T(128)S(1)} %copy-done.2, bf16[8,256,896]{2,1,0:T(8,128)(2,1)} %bitcast.37, bf16[896,512]{1,0:T(8,128)(2,1)S(1)} %copy-done.1), custom_call_target="tpu_custom_call" | custom-call | flops 1879048192 | bytes 7000000 | tf_op jit(solution)/shard_map/pallas_call | solution.py:134
  72.9 2.6 %collective-permute-start.4 = (bf16[8,8,16,512]{3,2,1,0:T(8,128)(2,1)S(1)}, bf16[8,8,16,512]{3,2,1,0:T(8,128)(2,1)S(1)}, u32[]{:S(2)}, u32[]{:S(2)}) collective-permute-start(bf16[8,8,16,512]{3,2,1,0:T(8,128)(2,1)S(1)} %get-tuple-element.45), channel_id=1, source_target_pairs={{0,32},{32,0},{1,33},{33,1},{2,34},{34,2},{3,35},{35,3},{4,36},{36... | collective-permute-start | bytes 3145736 | tf_op jit(solution)/shard_map/ppermute | solution.py:304
  75.5 4.1 %shard_map.70 = (bf16[128,896]{1,0:T(8,128)(2,1)S(1)}, bf16[128,896]{1,0:T(8,128)(2,1)S(1)}, bf16[128,896]{1,0:T(8,128)(2,1)S(1)}, bf16[128,896]{1,0:T(8,128)(2,1)S(1)}) custom-call(bf16[8,256,896]{2,1,0:T(8,128)(2,1)} %bitcast.38, bf16[8,256,512]{2,1,0:T(8,128)(2,1)S(1)} %copy-done), custom_call_target="tpu_custom_call" | custom-call | flops 1879048192 | bytes 7000000 | tf_op jit(solution)/shard_map/pallas_call | solution.py:187
  79.6 1.4 %add_convert_fusion = bf16[8,8,16,512]{3,2,1,0:T(8,128)(2,1)} fusion(bf16[8,8,16,512]{3,2,1,0:T(8,128)(2,1)S(1)} %collective-permute-done.4, bf16[8,8,16,512]{3,2,1,0:T(8,128)(2,1)S(1)} %get-tuple-element.44), kind=kLoop, calls=%fused_computation | loop fusion | flops 2097152 | bytes 3145728 | tf_op jit(solution)/shard_map/convert_element_type | solution.py:308
  81.1 5.1 %all-to-all-start.1 = ((bf16[8,8,16,512]{3,2,1,0:T(8,128)(2,1)}), bf16[8,8,16,512]{3,2,1,0:T(8,128)(2,1)S(1)}, u32[]{:S(2)}, u32[]{:S(2)}) async-start(bf16[8,8,16,512]{3,2,1,0:T(8,128)(2,1)} %add_convert_fusion), calls=%async_computation.1 | async-start | bytes 2097152 | tf_op jit(solution)/shard_map/all_to_all | solution.py:313
  86.1 7.1 %collective-permute-start.5 = (bf16[128,896]{1,0:T(8,128)(2,1)S(1)}, bf16[128,896]{1,0:T(8,128)(2,1)S(1)}, u32[]{:S(2)}, u32[]{:S(2)}) collective-permute-start(bf16[128,896]{1,0:T(8,128)(2,1)S(1)} %get-tuple-element.59), channel_id=1, source_target_pairs={{0,16},{8,24},{16,0},{24,8},{1,17},{9,25},{17,1},{25,9},{2,18},{10... | collective-permute-start | bytes 688136 | tf_op jit(solution)/shard_map/ppermute | solution.py:311
  93.2 2.7 %collective-permute-start.6 = (bf16[128,896]{1,0:T(8,128)(2,1)S(1)}, bf16[128,896]{1,0:T(8,128)(2,1)S(1)}, u32[]{:S(2)}, u32[]{:S(2)}) collective-permute-start(bf16[128,896]{1,0:T(8,128)(2,1)S(1)} %get-tuple-element.60), channel_id=1, source_target_pairs={{0,8},{8,16},{16,24},{24,0},{1,9},{9,17},{17,25},{25,1},{2,10},{10... | collective-permute-start | bytes 688136 | tf_op jit(solution)/shard_map/ppermute | solution.py:311
  95.9 4.7 %collective-permute-start.7 = (bf16[128,896]{1,0:T(8,128)(2,1)S(1)}, bf16[128,896]{1,0:T(8,128)(2,1)S(1)}, u32[]{:S(2)}, u32[]{:S(2)}) collective-permute-start(bf16[128,896]{1,0:T(8,128)(2,1)S(1)} %get-tuple-element.61), channel_id=1, source_target_pairs={{0,24},{8,0},{16,8},{24,16},{1,25},{9,1},{17,9},{25,17},{2,26},{10... | collective-permute-start | bytes 688136 | tf_op jit(solution)/shard_map/ppermute | solution.py:311
  100.6 0.5 all-to-all-done.1
  101.1 0.8 reduce_sum.12
  102.0 4.3 %all-to-all-start.2 = ((bf16[8,16,512]{2,1,0:T(8,128)(2,1)}), bf16[8,16,512]{2,1,0:T(8,128)(2,1)S(1)}, u32[]{:S(2)}, u32[]{:S(2)}) async-start(bf16[8,16,512]{2,1,0:T(8,128)(2,1)} %reduce_sum.12), calls=%async_computation.2 | async-start | bytes 262144 | tf_op jit(solution)/shard_map/all_to_all | solution.py:315
  106.3 2.3 %all-gather.8.cloned.1.call-done = s32[32,120,128]{2,1,0:T(8,128)} async-done(((s32[4,120,128]{2,1,0:T(8,128)}), s32[32,120,128]{2,1,0:T(8,128)}) %all-gather.8.cloned.1.call-update) | async-done | bytes 1966096 | tf_op jit(solution)/shard_map/all_gather | solution.py:318
  108.6 7.0 %shard_map.71 = bf16[256,896]{1,0:T(8,128)(2,1)} custom-call(bf16[256,4096]{1,0:T(8,128)(2,1)} %cot_ref.1, s32[8,4,120,128]{3,2,1,0:T(8,128)} %bitcast.39), custom_call_target="tpu_custom_call" | custom-call | flops 1879048192 | bytes 6000000 | tf_op jit(solution)/shard_map/pallas_call | solution.py:255
  115.6 6.4 %collective-permute-done.6 = bf16[128,896]{1,0:T(8,128)(2,1)S(1)} collective-permute-done((bf16[128,896]{1,0:T(8,128)(2,1)S(1)}, bf16[128,896]{1,0:T(8,128)(2,1)S(1)}, u32[]{:S(2)}, u32[]{:S(2)}) %collective-permute-start.6) | collective-permute-done | bytes 229408 | tf_op jit(solution)/shard_map/ppermute | solution.py:311
  122.2 1.0 copy.15
  123.3 0.7 copy.19
  (40 shorter events, 0.8 us)
Async XLA Ops:
  7.2 10.4 %copy-start.9 = (f32[7,1]{0,1:T(1,128)S(1)}, f32[7,1]{0,1:T(1,128)}, u32[]{:S(2)}) copy-start(f32[7,1]{0,1:T(1,128)} %param.7) | copy-start | bytes 88
  7.2 10.5 %copy-start.8 = (s32[224,128]{1,0:T(8,128)S(1)}, s32[224,128]{1,0:T(8,128)}, u32[]{:S(2)}) copy-start(s32[224,128]{1,0:T(8,128)} %param.6) | copy-start | bytes 344068
  7.2 60.7 %all-gather.6.cloned.1.call-start = ((), (), s32[]{:S(2)}) async-start(), calls=%async_computation.3 | async-start | bytes 4128768 | tf_op jit(solution)/shard_map/all_gather | solution.py:284
  9.9 26.2 %all-to-all-start = ((bf16[8,32,512]{2,1,0:T(8,128)(2,1)}), bf16[8,32,512]{2,1,0:T(8,128)(2,1)S(1)}, u32[]{:S(2)}, u32[]{:S(2)}) async-start(bf16[8,32,512]{2,1,0:T(8,128)(2,1)} %reshape.19), calls=%async_computation | async-start | bytes 524288 | tf_op jit(solution)/shard_map/all_to_all | solution.py:290
  17.5 91.0 %all-gather.8.cloned.1.call-start = ((), (), s32[]{:S(2)}) async-start(), calls=%async_computation.4 | async-start | bytes 2211840 | tf_op jit(solution)/shard_map/all_gather | solution.py:318
  36.1 25.6 %copy-start.3 = (bf16[8,32,512]{2,1,0:T(8,128)(2,1)}, bf16[8,32,512]{2,1,0:T(8,128)(2,1)S(1)}, u32[]{:S(2)}) copy-start(bf16[8,32,512]{2,1,0:T(8,128)(2,1)S(1)} %all-to-all-done.refs_0_) | copy-start | bytes 786436
  36.1 12.1 %collective-permute-start = (bf16[8,32,512]{2,1,0:T(8,128)(2,1)S(1)}, bf16[8,32,512]{2,1,0:T(8,128)(2,1)S(1)}, u32[]{:S(2)}, u32[]{:S(2)}) collective-permute-start(bf16[8,32,512]{2,1,0:T(8,128)(2,1)S(1)} %all-to-all-done.refs_0_), channel_id=1, source_target_pairs={{0,256},{64,320},{128,384},{192,448},{256,0},{320,64},{384,128},{4... | collective-permute-start | bytes 786440 | tf_op jit(solution)/shard_map/ppermute | solution.py:295
  39.9 8.3 %collective-permute-start.1 = (bf16[8,32,512]{2,1,0:T(8,128)(2,1)S(1)}, bf16[8,32,512]{2,1,0:T(8,128)(2,1)S(1)}, u32[]{:S(2)}, u32[]{:S(2)}) collective-permute-start(bf16[8,32,512]{2,1,0:T(8,128)(2,1)S(1)} %all-to-all-done.refs_0_), channel_id=1, source_target_pairs={{0,64},{64,0},{128,192},{192,128},{256,320},{320,256},{384,448},{4... | collective-permute-start | bytes 786440 | tf_op jit(solution)/shard_map/ppermute | solution.py:295
  43.0 8.5 %collective-permute-start.2 = (bf16[8,32,512]{2,1,0:T(8,128)(2,1)S(1)}, bf16[8,32,512]{2,1,0:T(8,128)(2,1)S(1)}, u32[]{:S(2)}, u32[]{:S(2)}) collective-permute-start(bf16[8,32,512]{2,1,0:T(8,128)(2,1)S(1)} %all-to-all-done.refs_0_), channel_id=1, source_target_pairs={{0,320},{64,256},{128,448},{192,384},{256,64},{320,0},{384,192},{4... | collective-permute-start | bytes 786440 | tf_op jit(solution)/shard_map/ppermute | solution.py:295
  48.2 13.5 %copy-start.5 = (bf16[8,32,512]{2,1,0:T(8,128)(2,1)}, bf16[8,32,512]{2,1,0:T(8,128)(2,1)S(1)}, u32[]{:S(2)}) copy-start(bf16[8,32,512]{2,1,0:T(8,128)(2,1)S(1)} %collective-permute-done.refs_1_) | copy-start | bytes 786436
  48.2 11.2 %copy-start.6 = (bf16[8,32,512]{2,1,0:T(8,128)(2,1)}, bf16[8,32,512]{2,1,0:T(8,128)(2,1)S(1)}, u32[]{:S(2)}) copy-start(bf16[8,32,512]{2,1,0:T(8,128)(2,1)S(1)} %collective-permute-done.1.refs_2_) | copy-start | bytes 786436
  51.5 8.0 %copy-start.7 = (bf16[8,32,512]{2,1,0:T(8,128)(2,1)}, bf16[8,32,512]{2,1,0:T(8,128)(2,1)S(1)}, u32[]{:S(2)}) copy-start(bf16[8,32,512]{2,1,0:T(8,128)(2,1)S(1)} %collective-permute-done.2.refs_3_) | copy-start | bytes 786436
  51.6 10.1 %collective-permute-start.3 = (bf16[4,8,32,512]{3,2,1,0:T(8,128)(2,1)S(1)}, bf16[4,8,32,512]{3,2,1,0:T(8,128)(2,1)S(1)}, u32[]{:S(2)}, u32[]{:S(2)}) collective-permute-start(bf16[4,8,32,512]{3,2,1,0:T(8,128)(2,1)S(1)} %pad_maximum_fusion), channel_id=1, source_target_pairs={{0,32},{32,0},{1,33},{33,1},{2,34},{34,2},{3,35},{35,3},{4,36},{36... | collective-permute-start | bytes 3145736 | tf_op jit(solution)/shard_map/ppermute | solution.py:299
  60.0 7.8 %copy-start.1 = (bf16[896,512]{1,0:T(8,128)(2,1)S(1)}, bf16[896,512]{1,0:T(8,128)(2,1)}, u32[]{:S(2)}) copy-start(bf16[896,512]{1,0:T(8,128)(2,1)} %shard_map.67.weight_ref) | copy-start | bytes 2752516
  60.0 7.8 %copy-start.2 = (s32[4]{0:T(128)S(1)}, s32[4]{0:T(128)}, u32[]{:S(2)}) copy-start(s32[4]{0:T(128)} %pad_add_fusion.1.place_ref) | copy-start | bytes 52
  61.7 1.0 copy-start.4
  67.8 7.7 %copy-start = (bf16[8,256,512]{2,1,0:T(8,128)(2,1)S(1)}, bf16[8,256,512]{2,1,0:T(8,128)(2,1)}, u32[]{:S(2)}) copy-start(bf16[8,256,512]{2,1,0:T(8,128)(2,1)} %shard_map.68.cot_ref) | copy-start | bytes 6291460
  72.9 6.7 %collective-permute-start.4 = (bf16[8,8,16,512]{3,2,1,0:T(8,128)(2,1)S(1)}, bf16[8,8,16,512]{3,2,1,0:T(8,128)(2,1)S(1)}, u32[]{:S(2)}, u32[]{:S(2)}) collective-permute-start(bf16[8,8,16,512]{3,2,1,0:T(8,128)(2,1)S(1)} %get-tuple-element.45), channel_id=1, source_target_pairs={{0,32},{32,0},{1,33},{33,1},{2,34},{34,2},{3,35},{35,3},{4,36},{36... | collective-permute-start | bytes 3145736 | tf_op jit(solution)/shard_map/ppermute | solution.py:304
  81.1 20.1 %all-to-all-start.1 = ((bf16[8,8,16,512]{3,2,1,0:T(8,128)(2,1)}), bf16[8,8,16,512]{3,2,1,0:T(8,128)(2,1)S(1)}, u32[]{:S(2)}, u32[]{:S(2)}) async-start(bf16[8,8,16,512]{3,2,1,0:T(8,128)(2,1)} %add_convert_fusion), calls=%async_computation.1 | async-start | bytes 2097152 | tf_op jit(solution)/shard_map/all_to_all | solution.py:313
  86.1 29.5 %collective-permute-start.5 = (bf16[128,896]{1,0:T(8,128)(2,1)S(1)}, bf16[128,896]{1,0:T(8,128)(2,1)S(1)}, u32[]{:S(2)}, u32[]{:S(2)}) collective-permute-start(bf16[128,896]{1,0:T(8,128)(2,1)S(1)} %get-tuple-element.59), channel_id=1, source_target_pairs={{0,16},{8,24},{16,0},{24,8},{1,17},{9,25},{17,1},{25,9},{2,18},{10... | collective-permute-start | bytes 688136 | tf_op jit(solution)/shard_map/ppermute | solution.py:311
  93.2 28.9 %collective-permute-start.6 = (bf16[128,896]{1,0:T(8,128)(2,1)S(1)}, bf16[128,896]{1,0:T(8,128)(2,1)S(1)}, u32[]{:S(2)}, u32[]{:S(2)}) collective-permute-start(bf16[128,896]{1,0:T(8,128)(2,1)S(1)} %get-tuple-element.60), channel_id=1, source_target_pairs={{0,8},{8,16},{16,24},{24,0},{1,9},{9,17},{17,25},{25,1},{2,10},{10... | collective-permute-start | bytes 688136 | tf_op jit(solution)/shard_map/ppermute | solution.py:311
  95.9 26.1 %collective-permute-start.7 = (bf16[128,896]{1,0:T(8,128)(2,1)S(1)}, bf16[128,896]{1,0:T(8,128)(2,1)S(1)}, u32[]{:S(2)}, u32[]{:S(2)}) collective-permute-start(bf16[128,896]{1,0:T(8,128)(2,1)S(1)} %get-tuple-element.61), channel_id=1, source_target_pairs={{0,24},{8,0},{16,8},{24,16},{1,25},{9,1},{17,9},{25,17},{2,26},{10... | collective-permute-start | bytes 688136 | tf_op jit(solution)/shard_map/ppermute | solution.py:311
  102.0 21.2 %all-to-all-start.2 = ((bf16[8,16,512]{2,1,0:T(8,128)(2,1)}), bf16[8,16,512]{2,1,0:T(8,128)(2,1)S(1)}, u32[]{:S(2)}, u32[]{:S(2)}) async-start(bf16[8,16,512]{2,1,0:T(8,128)(2,1)} %reduce_sum.12), calls=%async_computation.2 | async-start | bytes 262144 | tf_op jit(solution)/shard_map/all_to_all | solution.py:315
Sparse Core Ops, SparseCore 0:
  10.1 57.6 all-gather.5
  69.9 38.6 all-gather.7
